TPU v7x, 32 devices: a whole 2x2x4 slice. The times are simulated.
32 devices in a mesh: gx: 8 (over y, x, core), gy: 4 (over z).
Axes of the slice: x: 2, y: 2, z: 4, core: 2. Of those that a mesh axis runs over, the one named last changes fastest.
Arguments:
- stratum_warmth_celsius: float32 [50, 512, 512], P(None, 'gx', 'gy'), may hold values from -6 to 2
- stratum_mass_per_volume: float32 [50, 512, 512], P(None, 'gx', 'gy'), may hold values from 0.1 to 0.55
- stratum_melt_fluid: float32 [50, 512, 512], P(None, 'gx', 'gy'), may hold values from 0 to 0.04
- stratum_crystal_size: float32 [50, 512, 512], P(None, 'gx', 'gy'), may hold values from 0.2 to 2
- pile_stratum_tally: int32 [512, 512], P('gx', 'gy'), may hold values from 1 to 50, as said below
- pile_atmospheric_warmth: float32 [512, 512], P('gx', 'gy'), may hold values from -6 to 6
- topmost_thermal_factor: float32 [512, 512], P('gx', 'gy'), may hold values from 0.5 to 5
- movable_topmost_powder: float32 [512, 512], P('gx', 'gy'), may hold values from 0 to 1
- first_axis_gust_fraction: float32 [512, 512], P('gx', 'gy'), may hold values from -0.3 to 0.3
- second_axis_gust_fraction: float32 [512, 512], P('gx', 'gy'), may hold values from -0.3 to 0.3
- extra_stratum_warmth: float32 [50, 3072], P(None, ('gx', 'gy')), may hold values from -4 to 0
- extra_stratum_mass_per_volume: float32 [50, 3072], P(None, ('gx', 'gy')), may hold values from 0.4 to 0.8
- parent_pile: int32 [3072], P(('gx', 'gy')), may hold values from 0 to 262143, as said below
- pile_stream_segment: int32 [512, 512], P('gx', 'gy'), may hold values from 0 to 8191, as said below
- segment_result_index: int32 [131072], replicated, may hold values from 0 to 131071, as said below
Outputs:
- drift_final: float32 [512, 512], P('gx', 'gy')
- fresh_warmth: float32 [50, 512, 512], P(None, 'gx', 'gy')
- retained_fluid: float32 [50, 512, 512], P(None, 'gx', 'gy')
- extra_stratum_fresh_warmth: float32 [50, 3072], P(None, ('gx', 'gy'))
- segment_thaw_arrival: float32 [131072], P(('gx', 'gy'))
Inputs may be any that keep to these rules, and one draw needn't show every extreme that they name: `pile_stratum_tally`: columns named by parent_pile have 50 layers. `parent_pile`: no column is named twice. Of the 96 slots of one device at most 8 name columns of one tile, and one tile is named 8 times by the slots of every device. `pile_stream_segment`: codes of 4096 or more occur only in tiles with a + 1 < 8. segment_result_index is a permutation. Of the 4096 reaches t * 4096 to (t + 1) * 4096 - 1 of any tile t, exactly 128 have slots in each block h * 4096 to (h + 1) * 4096 - 1.
All inputs are finite; a program needn't handle non-finite values.
Results may differ from a plain program's by a relative error of at most 0.00002.
Values sent between devices are 32-bit elements; how exact they have to be, the bound alone decides.
A program may use at most 64 MiB of HBM per device.

v0:
```python
import functools

import jax
import jax.numpy as jnp
from jax import lax
from jax.experimental import pallas as pl
from jax.experimental.pallas import tpu as pltpu
from jax.sharding import PartitionSpec as P

STEPS = 4
PAIR = 8
LANES = 128

diffusion_number = 0.1
melt_rate = 0.02
holding_rate = 0.03

HIGH = lax.Precision.HIGHEST
NT = (((1,), (1,)), ((), ()))
TN = (((0,), (0,)), ((), ()))
NN = (((1,), (0,)), ((), ()))


def quotient(x, size):
    if size & (size - 1) == 0:
        return lax.shift_right_logical(x, jnp.full_like(x, size.bit_length() - 1))
    return lax.div(x, jnp.full_like(x, size))


def remainder(x, size):
    if size & (size - 1) == 0:
        return x & (size - 1)
    return lax.rem(x, jnp.full_like(x, size))


def rows_of(shape):
    return lax.broadcasted_iota(jnp.int32, shape, 0)


def lanes_of(shape):
    return lax.broadcasted_iota(jnp.int32, shape, 1)


def dot(a, b, dims, precision=None):
    return lax.dot_general(a, b, dims, precision=precision, preferred_element_type=jnp.float32)


def lane_chunk(i):
    return pl.ds(pl.multiple_of(i * LANES, LANES), LANES)


def fill_places(out_ref, index_ref, places, rows, unroll=4):
    def body(i, carry):
        hit = rows_of((places, LANES)) == index_ref[pl.ds(i, 1), :]
        out_ref[0:places, lane_chunk(i)] = jnp.where(hit, 1.0, 0.0).astype(jnp.bfloat16)
        return carry

    lax.fori_loop(0, rows, body, 0, unroll=unroll)


def fill_values(out_ref, index_ref, part_refs, places, rows, unroll=4):
    def body(i, carry):
        hit = rows_of((places, LANES)) == index_ref[pl.ds(i, 1), :]
        for p, part_ref in enumerate(part_refs):
            out_ref[p * places : (p + 1) * places, lane_chunk(i)] = jnp.where(
                hit, part_ref[pl.ds(i, 1), :], 0.0
            ).astype(jnp.bfloat16)
        return carry

    lax.fori_loop(0, rows, body, 0, unroll=unroll)


def split_three(value, part_refs):
    first = value.astype(jnp.bfloat16).astype(jnp.float32)
    second = (value - first).astype(jnp.bfloat16).astype(jnp.float32)
    part_refs[0][...] = first
    part_refs[1][...] = second
    part_refs[2][...] = value - first - second


def placed_sum(a_ref, b_ref, places, lanes, width, parts):
    both = dot(a_ref[0 : parts * places, 0:width], b_ref[0:lanes, 0:width], NT)
    return [both[p * places : (p + 1) * places] for p in range(parts)]


def deep_eliminate(temp_ref, rho_ref, elink_ref, dprime_ref, rprime_ref):
    layers = temp_ref.shape[0]
    kdeep = 1.0 + 24.0 * rho_ref[...] * rho_ref[...]
    elink_ref[0 : layers - 1, :] = 0.5 * (kdeep[:-1] + kdeep[1:])
    elink_ref[layers - 1 : layers, :] = jnp.zeros_like(kdeep[:1])
    elink = elink_ref[...]
    dprime_ref[...] = 1.0 + elink
    dprime_ref[1:layers, :] = dprime_ref[1:layers, :] + elink[:-1]
    last = pl.ds(layers - 1, 1)
    diag = dprime_ref[last, :] + kdeep[layers - 1 :]
    rhs = temp_ref[last, :]
    dprime_ref[last, :] = diag
    rprime_ref[last, :] = rhs

    def body(step, carry):
        diag, rhs = carry
        row = pl.ds(layers - 2 - step, 1)
        link = elink_ref[row, :]
        ratio = link / diag
        diag = dprime_ref[row, :] - link * ratio
        rhs = temp_ref[row, :] + ratio * rhs
        dprime_ref[row, :] = diag
        rprime_ref[row, :] = rhs
        return diag, rhs

    return lax.fori_loop(0, layers - 1, body, (diag, rhs), unroll=7)


def deep_positions(pile_row, pile_col, columns):
    slots = pile_row.shape[1]
    owner_row = quotient(pile_row, columns)
    owner_col = quotient(pile_col, columns)
    square = (slots, slots)
    earlier = (owner_row == owner_col) & (lanes_of(square) < rows_of(square))
    position = jnp.sum(jnp.where(earlier, 1.0, 0.0), axis=1, keepdims=True).astype(jnp.int32)
    return owner_row, owner_col, position


def as_column(row):
    size = row.shape[1]
    eye = rows_of((size, size)) == lanes_of((size, size))
    return jnp.sum(jnp.where(eye, row, 0.0), axis=1, keepdims=True)


def as_row(column):
    size = column.shape[0]
    eye = rows_of((size, size)) == lanes_of((size, size))
    return jnp.sum(jnp.where(eye, column, 0.0), axis=0, keepdims=True)


def deep_message(diag, rhs, pile_row, pile_col, columns, devices):
    owner_row, owner_col, position = deep_positions(pile_row, pile_col, columns)
    slots = pile_row.shape[1]
    lane = lanes_of((slots, LANES))
    cell = (remainder(pile_col, columns) + 1).astype(jnp.float32)
    table = jnp.where(lane == position, as_column(diag), 0.0)
    table = jnp.where(lane == position + PAIR, as_column(rhs), table)
    table = jnp.where(lane == position + 2 * PAIR, cell, table)
    pick = jnp.where(rows_of((devices, slots)) == owner_row, 1.0, 0.0)
    return dot(pick, table, NN, HIGH)


def ranks(holder_ref, rank_ref, hit_ref, count_ref, devices, rows):
    def fill(i, carry):
        hit = rows_of((devices, LANES)) == holder_ref[pl.ds(i, 1), :]
        place = pl.ds(pl.multiple_of(i * devices, devices), devices)
        hit_ref[place, :] = jnp.where(hit, 1.0, 0.0).astype(jnp.bfloat16)
        return carry

    lax.fori_loop(0, rows, fill, 0, unroll=4)
    shape = (LANES, 2 * LANES)
    before = (rows_of(shape) < lanes_of(shape)) | (lanes_of(shape) >= LANES)
    count_ref[...] = dot(hit_ref[...], jnp.where(before, 1.0, 0.0).astype(jnp.bfloat16), NN)

    def number(i, base):
        hit = rows_of((devices, LANES)) == holder_ref[pl.ds(i, 1), :]
        place = pl.ds(pl.multiple_of(i * devices, devices), devices)
        count = count_ref[place, 0:LANES] + base
        rank_ref[pl.ds(i, 1), :] = jnp.sum(
            jnp.where(hit, count, 0.0), axis=0, keepdims=True
        ).astype(jnp.int32)
        return base + count_ref[place, LANES : 2 * LANES]

    lax.fori_loop(0, rows, number, jnp.zeros((devices, LANES), jnp.float32), unroll=4)


def drift(snow, east, north, tile_x, tile_y, first_x, first_y, extent_x, extent_y, halo):
    shape = snow.shape
    x = rows_of(shape)
    y = lanes_of(shape)
    x = first_x + jnp.where(x >= tile_x + halo, x - shape[0], x)
    y = first_y + jnp.where(y >= tile_y + halo, y - shape[1], y)
    inside = (x >= 0) & (x < extent_x) & (y >= 0) & (y < extent_y)
    east_up, east_down = jnp.maximum(east, 0.0), jnp.minimum(east, 0.0)
    north_up, north_down = jnp.maximum(north, 0.0), jnp.minimum(north, 0.0)
    for step in range(STEPS):
        before_x = pltpu.roll(snow, 1, 0)
        after_x = pltpu.roll(snow, shape[0] - 1, 0)
        before_y = pltpu.roll(snow, 1, 1)
        after_y = pltpu.roll(snow, shape[1] - 1, 1)
        change = -east_up * (snow - before_x) - east_down * (after_x - snow)
        change = change - north_up * (snow - before_y) - north_down * (after_y - snow)
        snow = (
            snow
            + change
            + diffusion_number * (before_x + after_x + before_y + after_y - 4.0 * snow)
        )
        snow = jnp.where(inside, snow, 0.0)
    return snow[0:tile_x, 0:tile_y]


def deep_places(got, tile_x, tile_y):
    devices = got.shape[0]
    highs, lows, diags, rhss = [], [], [], []
    for k in range(PAIR):
        cell = got[:, 2 * PAIR + k : 2 * PAIR + k + 1].astype(jnp.int32) - 1
        full = cell >= 0
        cell = jnp.maximum(cell, 0)
        high = (lanes_of((devices, tile_x)) == quotient(cell, tile_y)) & full
        low = (lanes_of((devices, tile_y)) == remainder(cell, tile_y)) & full
        highs.append(jnp.where(high, 1.0, 0.0))
        low = jnp.where(low, 1.0, 0.0)
        lows.append(low)
        diags.append(low * got[:, k : k + 1])
        rhss.append(low * got[:, PAIR + k : PAIR + k + 1])
    high = jnp.concatenate(highs, axis=0)
    low = jnp.concatenate(lows, axis=0)
    table = jnp.concatenate(
        [jnp.concatenate(diags, axis=0), jnp.concatenate(rhss, axis=0), low], axis=1
    )
    dense = dot(high, table, TN, HIGH)
    return (
        high,
        low,
        dense[:, 0:tile_y],
        dense[:, tile_y : 2 * tile_y],
        dense[:, 2 * tile_y :],
    )


def deep_answers(high, low, dense, devices):
    found = dot(high, dense, NN, HIGH) * low
    lane = lanes_of((devices, LANES))
    answer = jnp.zeros((devices, LANES), jnp.float32)
    for k in range(PAIR):
        value = jnp.sum(found[k * devices : (k + 1) * devices], axis=1, keepdims=True)
        answer = jnp.where(lane == k, value, answer)
    return answer


def eliminate(temp_ref, rho_ref, size_ref, tally, exchange, air, ratio_ref, value_ref):
    layers = temp_ref.shape[0]

    def kappa_of(i):
        rho = rho_ref[i]
        return 1.0 + 24.0 * rho * rho * size_ref[i]

    def row(i, kappa, up, ratio, value, diag_more, rhs_more):
        kappa_next = kappa_of(i + 1)
        down = jnp.where(i + 1 < tally, 0.5 * (kappa + kappa_next), 0.0)
        diag = 1.0 + up + down + jnp.where(i == tally - 1, kappa, 0.0)
        rhs = temp_ref[i]
        if diag_more is not None:
            diag = diag + diag_more
            rhs = rhs + rhs_more
        inverse = 1.0 / (diag - up * ratio)
        value = (rhs + up * value) * inverse
        ratio = down * inverse
        ratio_ref[i] = ratio
        value_ref[i] = value
        return kappa_next, down, ratio, value

    zero = jnp.zeros_like(air)
    carry = row(0, kappa_of(0), zero, zero, zero, exchange, exchange * air)
    return lax.fori_loop(
        1, layers - 1, lambda i, c: row(i, *c, None, None), carry, unroll=2
    )


def bottom_row(temp_ref, tally, carry, base_diag, base_rhs, flag):
    layers = temp_ref.shape[0]
    kappa, up, ratio, value = carry
    scale = flag * kappa / (base_diag + kappa)
    diag = 1.0 + up + jnp.where(tally == layers, kappa, 0.0) - scale * kappa
    rhs = temp_ref[layers - 1] + scale * base_rhs
    bottom = (rhs + up * value) / (diag - up * ratio)
    surface_deep = (base_rhs + kappa * bottom) / (base_diag + kappa)
    return bottom, surface_deep


def substitute(fresh_ref, ratio_ref, value_ref, bottom):
    layers = fresh_ref.shape[0]
    fresh_ref[layers - 1] = bottom

    def body(step, below):
        i = layers - 2 - step
        below = value_ref[i] + ratio_ref[i] * below
        fresh_ref[i] = below
        return below

    lax.fori_loop(0, layers - 1, body, bottom, unroll=7)


def seep(fresh_ref, rho_ref, fluid_ref, tally, kept_ref):
    layers = fresh_ref.shape[0]

    def body(i, flux):
        live = i < tally
        source = fluid_ref[i] + melt_rate * jnp.maximum(fresh_ref[i], 0.0)
        avail = jnp.where(live, source, 0.0) + flux
        kept = jnp.where(live, jnp.minimum(avail, holding_rate * (1.0 - rho_ref[i])), 0.0)
        kept_ref[i] = kept
        return avail - kept

    return lax.fori_loop(0, layers, body, jnp.zeros(tally.shape, jnp.float32), unroll=5)


def deep_return(returned, owner_col, position, devices):
    slots = position.shape[0]
    pick = jnp.where(lanes_of((slots, devices)) == owner_col, 1.0, 0.0)
    found = dot(pick, returned, NN, HIGH)
    lane = lanes_of((slots, LANES))
    return as_row(jnp.sum(jnp.where(lane == position, found, 0.0), axis=1, keepdims=True))


def deep_substitute(first, elink_ref, dprime_ref, rprime_ref, out_ref):
    layers = out_ref.shape[0]
    inverse = 1.0 / dprime_ref[...]
    rprime_ref[...] = rprime_ref[...] * inverse
    dprime_ref[1:layers, :] = elink_ref[0 : layers - 1, :] * inverse[1:]
    out_ref[0:1, :] = first

    def body(j, above):
        row = pl.ds(j, 1)
        above = rprime_ref[row, :] + dprime_ref[row, :] * above
        out_ref[row, :] = above
        return above

    lax.fori_loop(1, layers, body, first, unroll=7)


def start_kernel(
    devices, columns, temp_ref, rho_ref, pile_row_ref, pile_col_ref, own_ref, next_ref,
    elink_ref, dprime_ref, rprime_ref, message_ref, own_rank_ref, next_rank_ref,
    holder_ref, hit_ref, count_ref, a_ref, b_ref, p0_ref, p1_ref,
):
    diag, rhs = deep_eliminate(temp_ref, rho_ref, elink_ref, dprime_ref, rprime_ref)
    message_ref[:, 0:LANES] = deep_message(
        diag, rhs, pile_row_ref[...], pile_col_ref[...], columns, devices
    )
    rows = own_ref.shape[0]
    reaches = rows * LANES
    peer = reaches // devices
    holder_ref[...] = quotient(next_ref[...], reaches)
    ranks(holder_ref, next_rank_ref, hit_ref, count_ref, devices, rows)
    holder_ref[...] = quotient(own_ref[...], reaches)
    ranks(holder_ref, own_rank_ref, hit_ref, count_ref, devices, rows)
    position = remainder(own_ref[...], reaches)
    p0_ref[...] = quotient(position, LANES).astype(jnp.float32)
    p1_ref[...] = remainder(position, LANES).astype(jnp.float32)
    fill_places(b_ref, own_rank_ref, peer, rows)
    fill_values(a_ref, holder_ref, (p0_ref, p1_ref), devices, rows)
    high, low = placed_sum(a_ref, b_ref, devices, peer, reaches, 2)
    message_ref[:, LANES : LANES + peer] = high * LANES + low


def middle_kernel(
    devices, extents, origin_ref, snow_ref, east_ref, north_ref, temp_ref, rho_ref, size_ref,
    fluid_ref, tally_ref, air_ref, factor_ref, code_ref, own_ref, next_ref, own_rank_ref,
    next_rank_ref, got_ref, drift_ref, fresh_ref, kept_ref, answer_ref, ratio_ref, value_ref,
    a_ref, b_ref, high_ref, low_ref, p0_ref, p1_ref, p2_ref,
):
    tile_x, tile_y = tally_ref.shape
    snow = drift(
        snow_ref[...], east_ref[...], north_ref[...], tile_x, tile_y,
        origin_ref[0], origin_ref[1], extents[0], extents[1], STEPS,
    )
    drift_ref[...] = snow
    exchange = factor_ref[...] / (1.0 + snow)
    tally = tally_ref[...]
    carry = eliminate(
        temp_ref, rho_ref, size_ref, tally, exchange, air_ref[...], ratio_ref, value_ref
    )
    high, low, base_diag, base_rhs, flag = deep_places(got_ref[...], tile_x, tile_y)
    bottom, surface_deep = bottom_row(temp_ref, tally, carry, base_diag, base_rhs, flag)
    answer_ref[:, 0:LANES] = deep_answers(high, low, surface_deep, devices)
    substitute(fresh_ref, ratio_ref, value_ref, bottom)
    runoff = seep(fresh_ref, rho_ref, fluid_ref, tally, kept_ref)
    rows = own_ref.shape[0]
    reaches = rows * LANES
    peer = reaches // devices
    parts = (p0_ref, p1_ref, p2_ref)
    split_three(runoff, parts)
    high_ref[...] = quotient(code_ref[...], LANES)
    low_ref[...] = remainder(code_ref[...], LANES)
    fill_places(b_ref, low_ref, LANES, tile_x)
    fill_values(a_ref, high_ref, parts, 2 * rows, tile_x)
    binned = sum(placed_sum(a_ref, b_ref, 2 * rows, LANES, tile_x * LANES, 3))
    split_three(binned, parts)
    for half, (slot_ref, rank_ref) in enumerate(((own_ref, own_rank_ref), (next_ref, next_rank_ref))):
        high_ref[0:rows, :] = quotient(slot_ref[...], reaches)
        fill_places(b_ref, rank_ref, peer, rows)
        halves = [p.at[pl.ds(half * rows, rows)] for p in parts]
        fill_values(a_ref, high_ref, halves, devices, rows)
        lane = LANES + half * peer
        answer_ref[:, lane : lane + peer] = sum(placed_sum(a_ref, b_ref, devices, peer, reaches, 3))


def end_kernel(
    devices, columns, returned_ref, pile_row_ref, pile_col_ref, elink_ref, dprime_in, rprime_in,
    value_ref, place_ref, deep_ref, arrival_ref, dprime_ref, rprime_ref, a_ref, b_ref, high_ref,
    low_ref, p0_ref, p1_ref, p2_ref,
):
    owner_row, owner_col, position = deep_positions(pile_row_ref[...], pile_col_ref[...], columns)
    first = deep_return(returned_ref[...], owner_col, position, devices)
    dprime_ref[...] = dprime_in[...]
    rprime_ref[...] = rprime_in[...]
    deep_substitute(first, elink_ref, dprime_ref, rprime_ref, deep_ref)
    rows = value_ref.shape[0]
    parts = (p0_ref, p1_ref, p2_ref)
    split_three(value_ref[...], parts)
    place = place_ref[...]
    high_ref[...] = quotient(place, LANES)
    low_ref[...] = remainder(place, LANES)
    fill_places(b_ref, low_ref, LANES, rows)
    fill_values(a_ref, high_ref, parts, rows, rows)
    arrival_ref[...] = sum(placed_sum(a_ref, b_ref, rows, LANES, rows * LANES, 3))


def call(kernel, outs, scratch, smem_first=False):
    def run(*args):
        specs = [pl.BlockSpec(memory_space=pltpu.VMEM)] * len(args)
        if smem_first:
            specs[0] = pl.BlockSpec(memory_space=pltpu.SMEM)
        return pl.pallas_call(
            kernel,
            out_shape=[jax.ShapeDtypeStruct(s, d) for s, d in outs],
            in_specs=specs,
            out_specs=[pl.BlockSpec(memory_space=pltpu.VMEM)] * len(outs),
            scratch_shapes=[pltpu.VMEM(s, d) for s, d in scratch],
            compiler_params=pltpu.CompilerParams(vmem_limit_bytes=48 * 2**20),
        )(*args)

    return run


def halo_of(cells, axis, dim, width):
    count = lax.axis_size(axis)
    head = lax.slice_in_dim(cells, 0, width, axis=dim)
    tail = lax.slice_in_dim(cells, cells.shape[dim] - width, cells.shape[dim], axis=dim)
    before = lax.ppermute(tail, axis, [(i, i + 1) for i in range(count - 1)])
    after = lax.ppermute(head, axis, [(i + 1, i) for i in range(count - 1)])
    gap = list(cells.shape)
    gap[dim] = (-(cells.shape[dim] + 2 * width)) % (LANES if dim == 2 else 8)
    return jnp.concatenate([cells, after, jnp.zeros(gap, cells.dtype), before], axis=dim)


def local(
    stratum_warmth_celsius,
    stratum_mass_per_volume,
    stratum_melt_fluid,
    stratum_crystal_size,
    pile_stratum_tally,
    pile_atmospheric_warmth,
    topmost_thermal_factor,
    movable_topmost_powder,
    first_axis_gust_fraction,
    second_axis_gust_fraction,
    extra_stratum_warmth,
    extra_stratum_mass_per_volume,
    parent_pile,
    pile_stream_segment,
    segment_result_index,
):
    f32, i32, bf16 = jnp.float32, jnp.int32, jnp.bfloat16
    layers, tile_x, tile_y = stratum_warmth_celsius.shape
    deep_layers, slots = extra_stratum_warmth.shape
    tiles_x = lax.axis_size("gx")
    tiles_y = lax.axis_size("gy")
    devices = tiles_x * tiles_y
    columns = tile_x * tile_y
    reaches = segment_result_index.shape[0] // devices
    rows = reaches // LANES
    peer = reaches // devices
    extents = (tile_x * tiles_x, tile_y * tiles_y)
    gx, gy = lax.axis_index("gx"), lax.axis_index("gy")
    tile = gx * tiles_y + gy
    after = jnp.minimum(gx + 1, tiles_x - 1) * tiles_y + gy
    index = segment_result_index.reshape(devices * rows, LANES)
    own = lax.dynamic_slice_in_dim(index, tile * rows, rows, axis=0)
    following = lax.dynamic_slice_in_dim(index, after * rows, rows, axis=0)
    pile_row = parent_pile.reshape(1, slots)
    pile_col = parent_pile.reshape(slots, 1)

    fields = jnp.stack([movable_topmost_powder, first_axis_gust_fraction, second_axis_gust_fraction])
    fields = halo_of(fields, "gx", 1, STEPS)
    fields = halo_of(fields, "gy", 2, STEPS)

    wide = max(3 * 2 * rows, 3 * devices)
    elink, dprime, rprime, message, own_rank, next_rank = call(
        functools.partial(start_kernel, devices, columns),
        [((deep_layers, slots), f32)] * 3
        + [((devices, LANES + peer), f32), ((rows, LANES), i32), ((rows, LANES), i32)],
        [
            ((rows, LANES), i32),
            ((rows * devices, LANES), bf16),
            ((rows * devices, 2 * LANES), f32),
            ((2 * devices, reaches), bf16),
            ((peer, reaches), bf16),
            ((rows, LANES), f32),
            ((rows, LANES), f32),
        ],
    )(extra_stratum_warmth, extra_stratum_mass_per_volume, pile_row, pile_col, own, following)
    got = lax.all_to_all(message, ("gx", "gy"), split_axis=0, concat_axis=0, tiled=True)
    origin = jnp.stack([gx * tile_x, gy * tile_y]).astype(i32)
    drift_final, fresh, kept, answer = call(
        functools.partial(middle_kernel, devices, extents),
        [
            ((tile_x, tile_y), f32),
            ((layers, tile_x, tile_y), f32),
            ((layers, tile_x, tile_y), f32),
            ((devices, LANES + 2 * peer), f32),
        ],
        [
            ((layers, tile_x, tile_y), f32),
            ((layers, tile_x, tile_y), f32),
            ((wide, columns), bf16),
            ((LANES, columns), bf16),
            ((tile_x, LANES), i32),
            ((tile_x, LANES), i32),
        ]
        + [((tile_x, LANES), f32)] * 3,
        smem_first=True,
    )(
        origin, fields[0], fields[1], fields[2], stratum_warmth_celsius, stratum_mass_per_volume,
        stratum_crystal_size, stratum_melt_fluid, pile_stratum_tally, pile_atmospheric_warmth,
        topmost_thermal_factor, pile_stream_segment, own, following, own_rank, next_rank,
        got[:, 0:LANES],
    )
    back = lax.all_to_all(answer, ("gx", "gy"), split_axis=0, concat_axis=0, tiled=True)
    straight = back[:, LANES : LANES + peer]
    shifted = back[: devices - tiles_y, LANES + peer :]
    total = straight + jnp.pad(shifted, ((tiles_y, 0), (0, 0)))
    place = got[:, LANES:].astype(i32)
    deep_fresh, arrival = call(
        functools.partial(end_kernel, devices, columns),
        [((deep_layers, slots), f32), ((rows, LANES), f32)],
        [
            ((deep_layers, slots), f32),
            ((deep_layers, slots), f32),
            ((3 * rows, reaches), bf16),
            ((LANES, reaches), bf16),
            ((rows, LANES), i32),
            ((rows, LANES), i32),
        ]
        + [((rows, LANES), f32)] * 3,
    )(
        back[:, 0:LANES], pile_row, pile_col, elink, dprime, rprime,
        total.reshape(rows, LANES), place.reshape(rows, LANES),
    )
    return drift_final, fresh, kept, deep_fresh, arrival.reshape(reaches)


def solution(mesh):
    cells = P("gx", "gy")
    strata = P(None, "gx", "gy")
    deep = P(None, ("gx", "gy"))
    return jax.shard_map(
        local,
        mesh=mesh,
        in_specs=(strata,) * 4 + (cells,) * 6 + (deep, deep, P(("gx", "gy")), cells, P()),
        out_specs=(cells, strata, strata, deep, P(("gx", "gy"))),
        check_vma=False,
    )
```

profile of v0, /device:TPU:0, one launch (start us, length us, event | category | flops | bytes accessed | tf_op | source)
XLA Modules:
  0.0 63.3 jit_solution(17413049144820052651)
XLA Ops:
  0.6 0.0 copy-start.6
  0.6 0.0 copy-start.5
  0.7 0.0 copy-start.4
  0.7 0.0 copy-start.3
  0.7 0.0 copy-start
  0.7 0.9 %pad_maximum_fusion.4 = (f32[3,4,128]{2,1,0:T(4,128)S(1)}, f32[3,4,128]{2,1,0:T(4,128)S(1)}) fusion(f32[1,64,128]{2,1,0:T(8,128)} %bitcast.28, f32[1,64,128]{2,1,0:T(8,128)} %bitcast.31, f32[1,64,128]{2,1,0:T(8,128)} %bitcast.34), kind=kLoop, calls=%fused_computation.11 | loop fusion | flops 6144 | bytes 110592 | tf_op jit(solution)/shard_map/slice | solution.py:434
  1.6 1.3 %collective-permute-start = (f32[3,4,128]{2,1,0:T(4,128)S(1)}, f32[3,4,128]{2,1,0:T(4,128)S(1)}, u32[]{:S(2)}, u32[]{:S(2)}) collective-permute-start(f32[3,4,128]{2,1,0:T(4,128)S(1)} %get-tuple-element.36), channel_id=1, source_target_pairs={{4,0},{8,4},{12,8},{16,12},{20,16},{24,20},{28,24},{5,1},{9,5},{13... | collective-permute-start | bytes 18440 | tf_op jit(solution)/shard_map/ppermute | solution.py:437
  2.9 3.0 %collective-permute-start.1 = (f32[3,4,128]{2,1,0:T(4,128)S(1)}, f32[3,4,128]{2,1,0:T(4,128)S(1)}, u32[]{:S(2)}, u32[]{:S(2)}) collective-permute-start(f32[3,4,128]{2,1,0:T(4,128)S(1)} %get-tuple-element.37), channel_id=1, source_target_pairs={{0,4},{4,8},{8,12},{12,16},{16,20},{20,24},{24,28},{1,5},{5,9},{9,... | collective-permute-start | bytes 18440 | tf_op jit(solution)/shard_map/ppermute | solution.py:436
  5.9 0.7 %constant_dynamic-slice_fusion = (s32[32,128]{1,0:T(8,128)S(1)}, s32[32,128]{1,0:T(8,128)S(1)}) fusion(s32[1024,128]{1,0:T(8,128)} %bitcast.40, s32[]{:T(128)S(6)} %select_n.7, s32[]{:T(128)S(6)} %select_n.6), kind=kLoop, calls=%fused_computation.13 | loop fusion | bytes 65544 | tf_op jit(solution)/shard_map/dynamic_slice | solution.py:476
  6.7 0.8 %copy.22.pile_col_ref = s32[96,1]{1,0:T(8,128)S(1)} copy(s32[96,1]{0,1:T(1,128)} %bitcast.25) | data formatting | bytes 768 | tf_op jit(solution)/shard_map/reshape | solution.py:478
  7.4 0.0 copy-start.7
  7.4 0.7 %copy-done.7 = f32[50,96]{1,0:T(8,128)S(1)} copy-done((f32[50,96]{1,0:T(8,128)S(1)}, f32[50,96]{1,0:T(8,128)}, u32[]{:S(2)}) %copy-start.7) | copy-done | bytes 19224
  8.2 0.0 copy-start.8
  8.2 0.7 %copy-done.8 = f32[50,96]{1,0:T(8,128)S(1)} copy-done((f32[50,96]{1,0:T(8,128)S(1)}, f32[50,96]{1,0:T(8,128)}, u32[]{:S(2)}) %copy-start.8) | copy-done | bytes 19224
  8.9 0.0 copy-start.9
  8.9 0.7 %copy-done.9 = s32[96]{0:T(128)S(1)} copy-done((s32[96]{0:T(128)S(1)}, s32[96]{0:T(128)}, u32[]{:S(2)}) %copy-start.9) | copy-done | bytes 408
  9.6 3.4 %shard_map.182 = (f32[50,96]{1,0:T(8,128)S(1)}, f32[50,96]{1,0:T(8,128)S(1)}, f32[50,96]{1,0:T(8,128)S(1)}, f32[32,256]{1,0:T(8,128)S(1)}, s32[32,128]{1,0:T(8,128)S(1)}, /*index=5*/s32[32,128]{1,0:T(8,128)S(1)}) custom-call(f32[50,96]{1,0:T(8,128)S(1)} %copy-done.7, f32[50,96]{1,0:T(8,128)S(1)} %copy-done.8, s32[1,96]{1,0:T(1,128)S(1)} %bitcast.26, ...), custom_call_target="tpu_custom_call" | custom-call | tf_op jit(solution)/shard_map/pallas_call | solution.py:420
  12.9 0.7 %copy.23 = f32[32,1,256]{2,1,0:T(1,128)} copy(f32[32,1,256]{2,0,1:T(8,128)S(1)} %bitcast.24) | data formatting | bytes 65536 | tf_op jit(solution)/shard_map/all_to_all | solution.py:499
  13.6 7.9 %all-to-all-start = ((f32[32,1,256]{2,1,0:T(1,128)}), f32[32,1,256]{2,1,0:T(1,128)S(1)}, u32[]{:S(2)}, u32[]{:S(2)}) async-start(f32[32,1,256]{2,1,0:T(1,128)} %copy.23), calls=%async_computation | async-start | bytes 65536 | tf_op jit(solution)/shard_map/all_to_all | solution.py:499
  21.5 0.0 collective-permute-done
  21.5 0.0 collective-permute-done.1
  21.5 0.8 %pad_maximum_fusion.1 = f32[3,72,128]{2,1,0:T(8,128)S(1)} fusion(f32[3,4,128]{2,1,0:T(4,128)S(1)} %collective-permute-done.1, f32[3,4,128]{2,1,0:T(4,128)S(1)} %collective-permute-done, f32[1,64,128]{2,1,0:T(8,128)} %bitcast.29, f32[1,64,128]{2,1,0:T(8,128)} %bitcast.32, f32[1,64,128]{2,1,0:T(8,128)} %bitcast.35), kind=kLoop, calls=%fused_computation.1 | loop fusion | flops 110592 | bytes 221184 | tf_op jit(solution)/shard_map/concatenate | solution.py:440
  22.3 0.1 fusion
  22.4 1.3 %collective-permute-start.2 = (f32[3,72,4]{2,1,0:T(8,128)S(1)}, f32[3,72,4]{2,1,0:T(8,128)S(1)}, u32[]{:S(2)}, u32[]{:S(2)}) collective-permute-start(f32[3,72,4]{2,1,0:T(8,128)S(1)} %get-tuple-element.34), channel_id=1, source_target_pairs={{1,0},{2,1},{3,2},{5,4},{6,5},{7,6},{9,8},{10,9},{11,10},{13,12},{... | collective-permute-start | bytes 10376 | tf_op jit(solution)/shard_map/ppermute | solution.py:437
  23.7 4.6 %collective-permute-start.3 = (f32[3,72,4]{2,1,0:T(8,128)S(1)}, f32[3,72,4]{2,1,0:T(8,128)S(1)}, u32[]{:S(2)}, u32[]{:S(2)}) collective-permute-start(f32[3,72,4]{2,1,0:T(8,128)S(1)} %get-tuple-element.35), channel_id=1, source_target_pairs={{0,1},{1,2},{2,3},{4,5},{5,6},{6,7},{8,9},{9,10},{10,11},{12,13},{... | collective-permute-start | bytes 10376 | tf_op jit(solution)/shard_map/ppermute | solution.py:436
  28.3 0.1 pad_add_fusion.origin_ref
  28.4 0.1 pad.11.clone
  28.5 1.1 %collective-permute-done.2 = f32[3,72,4]{2,1,0:T(8,128)S(1)} collective-permute-done((f32[3,72,4]{2,1,0:T(8,128)S(1)}, f32[3,72,4]{2,1,0:T(8,128)S(1)}, u32[]{:S(2)}, u32[]{:S(2)}) %collective-permute-start.2) | collective-permute-done | bytes 3488 | tf_op jit(solution)/shard_map/ppermute | solution.py:437
  29.5 1.2 %collective-permute-done.3 = f32[3,72,4]{2,1,0:T(8,128)S(1)} collective-permute-done((f32[3,72,4]{2,1,0:T(8,128)S(1)}, f32[3,72,4]{2,1,0:T(8,128)S(1)}, u32[]{:S(2)}, u32[]{:S(2)}) %collective-permute-start.3) | collective-permute-done | bytes 3488 | tf_op jit(solution)/shard_map/ppermute | solution.py:436
  30.7 0.9 %pad_maximum_fusion = f32[3,72,256]{2,1,0:T(8,128)S(1)} fusion(f32[3,72,4]{2,1,0:T(8,128)S(1)} %collective-permute-done.3, f32[3,72,4]{2,1,0:T(8,128)S(1)} %collective-permute-done.2, f32[3,4,128]{2,1,0:T(4,128)S(1)} %collective-permute-done.1, f32[3,4,128]{2,1,0:T(4,128)S(1)} %collective-permute-done, f32[1,64,128]{2,1,0:T(8,128)} %bitcast.30, ...), kind=kLoop, calls=%fused_computation | loop fusion | flops 387072 | bytes 339712 | tf_op jit(solution)/shard_map/concatenate | solution.py:440
  31.6 0.0 all-to-all-done
  31.7 0.0 copy-done.6
  31.7 0.0 copy-done.5
  31.7 0.0 copy-done.4
  31.7 0.0 copy-done.3
  31.7 0.0 copy-done
  31.7 0.0 copy-start.1
  31.7 1.4 %copy-done.1 = f32[50,64,128]{2,1,0:T(8,128)S(1)} copy-done((f32[50,64,128]{2,1,0:T(8,128)S(1)}, f32[50,64,128]{2,1,0:T(8,128)}, u32[]{:S(2)}) %copy-start.1) | copy-done | bytes 1638424
  33.2 0.0 copy-start.2
  33.2 1.4 %copy-done.2 = f32[50,64,128]{2,1,0:T(8,128)S(1)} copy-done((f32[50,64,128]{2,1,0:T(8,128)S(1)}, f32[50,64,128]{2,1,0:T(8,128)}, u32[]{:S(2)}) %copy-start.2) | copy-done | bytes 1638424
  34.6 0.0 copy-start.10
  34.6 12.5 %shard_map.183 = (f32[64,128]{1,0:T(8,128)}, f32[50,64,128]{2,1,0:T(8,128)}, f32[50,64,128]{2,1,0:T(8,128)}, f32[32,384]{1,0:T(8,128)S(1)}) custom-call(s32[2]{0:T(128)S(1)} %pad_add_fusion.origin_ref, f32[72,256]{1,0:T(8,128)S(1)} %get-tuple-element.33.snow_ref, f32[72,256]{1,0:T(8,128)S(1)} %get-tuple-element.32.east_ref, ...), custom_call_target="tpu_custom_call" | custom-call | tf_op jit(solution)/shard_map/pallas_call | solution.py:420
  47.1 0.1 copy.24
  47.2 13.9 %all_to_all.24 = f32[32,1,384]{2,1,0:T(1,128)S(1)} all-to-all(f32[32,1,384]{2,1,0:T(1,128)S(1)} %copy.24), channel_id=1, replica_groups=mesh['gx'=8,'gy'=4] {'gx','gy'}, dimensions={0} | all-to-all | bytes 98304 | tf_op jit(solution)/shard_map/all_to_all | solution.py:525
  61.1 0.0 copy-done.10
  61.1 2.2 %shard_map.184 = (f32[50,96]{1,0:T(8,128)}, f32[32,128]{1,0:T(8,128)}) custom-call(f32[32,128]{1,0:T(8,128)S(1)} %get-tuple-element.39.returned_ref, s32[1,96]{1,0:T(1,128)S(1)} %bitcast.27, s32[96,1]{1,0:T(8,128)S(1)} %copy.22.pile_col_ref, f32[50,96]{1,0:T(8,128)S(1)} %get-tuple-element.24.elink_ref, f32[50,96]{1,0:T(8,128)S(1)} %get-tuple-element.25.dprime_in, ...), custom_call_target="tpu_custom_call" | custom-call | tf_op jit(solution)/shard_map/pallas_call | solution.py:420
  (7 shorter events, 0.0 us)
Async XLA Ops:
  0.6 31.0 %copy-start.6 = (s32[64,128]{1,0:T(8,128)S(1)}, s32[64,128]{1,0:T(8,128)}, u32[]{:S(2)}) copy-start(s32[64,128]{1,0:T(8,128)} %code_ref.1) | copy-start | bytes 98308
  0.6 31.0 %copy-start.5 = (f32[64,128]{1,0:T(8,128)S(1)}, f32[64,128]{1,0:T(8,128)}, u32[]{:S(2)}) copy-start(f32[64,128]{1,0:T(8,128)} %factor_ref.1) | copy-start | bytes 98308
  0.7 31.0 %copy-start.4 = (f32[64,128]{1,0:T(8,128)S(1)}, f32[64,128]{1,0:T(8,128)}, u32[]{:S(2)}) copy-start(f32[64,128]{1,0:T(8,128)} %air_ref.1) | copy-start | bytes 98308
  0.7 31.0 %copy-start.3 = (s32[64,128]{1,0:T(8,128)S(1)}, s32[64,128]{1,0:T(8,128)}, u32[]{:S(2)}) copy-start(s32[64,128]{1,0:T(8,128)} %tally_ref.1) | copy-start | bytes 98308
  0.7 31.0 %copy-start = (f32[50,64,128]{2,1,0:T(8,128)S(1)}, f32[50,64,128]{2,1,0:T(8,128)}, u32[]{:S(2)}) copy-start(f32[50,64,128]{2,1,0:T(8,128)} %temp_ref.3) | copy-start | bytes 4915204
  1.6 19.9 %collective-permute-start = (f32[3,4,128]{2,1,0:T(4,128)S(1)}, f32[3,4,128]{2,1,0:T(4,128)S(1)}, u32[]{:S(2)}, u32[]{:S(2)}) collective-permute-start(f32[3,4,128]{2,1,0:T(4,128)S(1)} %get-tuple-element.36), channel_id=1, source_target_pairs={{4,0},{8,4},{12,8},{16,12},{20,16},{24,20},{28,24},{5,1},{9,5},{13... | collective-permute-start | bytes 18440 | tf_op jit(solution)/shard_map/ppermute | solution.py:437
  2.9 18.7 %collective-permute-start.1 = (f32[3,4,128]{2,1,0:T(4,128)S(1)}, f32[3,4,128]{2,1,0:T(4,128)S(1)}, u32[]{:S(2)}, u32[]{:S(2)}) collective-permute-start(f32[3,4,128]{2,1,0:T(4,128)S(1)} %get-tuple-element.37), channel_id=1, source_target_pairs={{0,4},{4,8},{8,12},{12,16},{16,20},{20,24},{24,28},{1,5},{5,9},{9,... | collective-permute-start | bytes 18440 | tf_op jit(solution)/shard_map/ppermute | solution.py:436
  7.4 0.7 %copy-start.7 = (f32[50,96]{1,0:T(8,128)S(1)}, f32[50,96]{1,0:T(8,128)}, u32[]{:S(2)}) copy-start(f32[50,96]{1,0:T(8,128)} %temp_ref.2) | copy-start | bytes 57604
  8.2 0.7 %copy-start.8 = (f32[50,96]{1,0:T(8,128)S(1)}, f32[50,96]{1,0:T(8,128)}, u32[]{:S(2)}) copy-start(f32[50,96]{1,0:T(8,128)} %rho_ref.2) | copy-start | bytes 57604
  8.9 0.7 %copy-start.9 = (s32[96]{0:T(128)S(1)}, s32[96]{0:T(128)}, u32[]{:S(2)}) copy-start(s32[96]{0:T(128)} %param.27) | copy-start | bytes 1156
  13.6 18.1 %all-to-all-start = ((f32[32,1,256]{2,1,0:T(1,128)}), f32[32,1,256]{2,1,0:T(1,128)S(1)}, u32[]{:S(2)}, u32[]{:S(2)}) async-start(f32[32,1,256]{2,1,0:T(1,128)} %copy.23), calls=%async_computation | async-start | bytes 65536 | tf_op jit(solution)/shard_map/all_to_all | solution.py:499
  22.4 7.1 %collective-permute-start.2 = (f32[3,72,4]{2,1,0:T(8,128)S(1)}, f32[3,72,4]{2,1,0:T(8,128)S(1)}, u32[]{:S(2)}, u32[]{:S(2)}) collective-permute-start(f32[3,72,4]{2,1,0:T(8,128)S(1)} %get-tuple-element.34), channel_id=1, source_target_pairs={{1,0},{2,1},{3,2},{5,4},{6,5},{7,6},{9,8},{10,9},{11,10},{13,12},{... | collective-permute-start | bytes 10376 | tf_op jit(solution)/shard_map/ppermute | solution.py:437
  23.7 7.0 %collective-permute-start.3 = (f32[3,72,4]{2,1,0:T(8,128)S(1)}, f32[3,72,4]{2,1,0:T(8,128)S(1)}, u32[]{:S(2)}, u32[]{:S(2)}) collective-permute-start(f32[3,72,4]{2,1,0:T(8,128)S(1)} %get-tuple-element.35), channel_id=1, source_target_pairs={{0,1},{1,2},{2,3},{4,5},{5,6},{6,7},{8,9},{9,10},{10,11},{12,13},{... | collective-permute-start | bytes 10376 | tf_op jit(solution)/shard_map/ppermute | solution.py:436
  31.7 1.4 %copy-start.1 = (f32[50,64,128]{2,1,0:T(8,128)S(1)}, f32[50,64,128]{2,1,0:T(8,128)}, u32[]{:S(2)}) copy-start(f32[50,64,128]{2,1,0:T(8,128)} %rho_ref.3) | copy-start | bytes 4915204
  33.2 1.4 %copy-start.2 = (f32[50,64,128]{2,1,0:T(8,128)S(1)}, f32[50,64,128]{2,1,0:T(8,128)}, u32[]{:S(2)}) copy-start(f32[50,64,128]{2,1,0:T(8,128)} %size_ref.1) | copy-start | bytes 4915204
  34.6 26.5 %copy-start.10 = (s32[96]{0:T(128)S(1)}, s32[96]{0:T(128)}, u32[]{:S(2)}) copy-start(s32[96]{0:T(128)} %param.27) | copy-start | bytes 1156
where the time goes:
time: 64 us; the launch traced here: 63.3 us
  starting transfers between devices  18.1 us (28%)
  Pallas kernels  18.1 us (28%)
  blocking collectives  13.9 us (22%)
  local copies, waits for them, and re-layouts  7.42 us (12%)
  other arithmetic  2.69 us (4%)
  waiting for transfers between devices  2.28 us (4%)
  between operations  0.86 us (1%)
    pallas_call x3, Pallas kernels, run(): pl.pallas_call(kernel, out_shape=[jax.ShapeDtypeStruct(s, d) for s, d in...  18.1 us
    all_to_all x1, blocking collectives, local(): lax.all_to_all(answer, ('gx', 'gy'), split_axis=0, concat_axis=0, tiled=T...  13.9 us
    all_to_all x1, starting transfers between devices, local(): lax.all_to_all(message, ('gx', 'gy'), split_axis=0, concat_axis=0, tiled=...  7.91 us
    ppermute x2, starting transfers between devices, halo_of(): before = lax.ppermute(tail, axis, [(i, i + 1) for i in range(count - 1)])  7.58 us
    unnamed x24, local copies, waits for them, and re-layouts  5.03 us
    ppermute x2, starting transfers between devices, halo_of(): after = lax.ppermute(head, axis, [(i + 1, i) for i in range(count - 1)])  2.57 us
    concatenate x2, other arithmetic, halo_of(): jnp.concatenate([cells, after, jnp.zeros(gap, cells.dtype), before], axis...  1.69 us
  transfers between devices with their start and end apart: 5, of which 2 were waited for; matrix products, arithmetic and copies ran while one was open for 6% of the time, Pallas kernels for 5%

commit v1 on v0

--- a/solution.py
+++ b/solution.py
@@ -73,9 +73,10 @@
 def split_three(value, part_refs):
     first = value.astype(jnp.bfloat16).astype(jnp.float32)
     second = (value - first).astype(jnp.bfloat16).astype(jnp.float32)
-    part_refs[0][...] = first
-    part_refs[1][...] = second
-    part_refs[2][...] = value - first - second
+    rows = value.shape[0]
+    part_refs[0][0:rows, :] = first
+    part_refs[1][0:rows, :] = second
+    part_refs[2][0:rows, :] = value - first - second
 
 
 def placed_sum(a_ref, b_ref, places, lanes, width, parts):
@@ -111,14 +112,15 @@
     return lax.fori_loop(0, layers - 1, body, (diag, rhs), unroll=7)
 
 
-def deep_positions(pile_row, pile_col, columns):
+def deep_positions(pile_row, columns):
     slots = pile_row.shape[1]
+    pile_col = as_column(pile_row.astype(jnp.float32)).astype(jnp.int32)
     owner_row = quotient(pile_row, columns)
     owner_col = quotient(pile_col, columns)
     square = (slots, slots)
     earlier = (owner_row == owner_col) & (lanes_of(square) < rows_of(square))
     position = jnp.sum(jnp.where(earlier, 1.0, 0.0), axis=1, keepdims=True).astype(jnp.int32)
-    return owner_row, owner_col, position
+    return owner_row, owner_col, remainder(pile_col, columns), position
 
 
 def as_column(row):
@@ -133,11 +135,10 @@
     return jnp.sum(jnp.where(eye, column, 0.0), axis=0, keepdims=True)
 
 
-def deep_message(diag, rhs, pile_row, pile_col, columns, devices):
-    owner_row, owner_col, position = deep_positions(pile_row, pile_col, columns)
-    slots = pile_row.shape[1]
+def deep_message(diag, rhs, owner_row, cell, position, devices):
+    slots = owner_row.shape[1]
     lane = lanes_of((slots, LANES))
-    cell = (remainder(pile_col, columns) + 1).astype(jnp.float32)
+    cell = (cell + 1).astype(jnp.float32)
     table = jnp.where(lane == position, as_column(diag), 0.0)
     table = jnp.where(lane == position + PAIR, as_column(rhs), table)
     table = jnp.where(lane == position + 2 * PAIR, cell, table)
@@ -178,6 +179,7 @@
     inside = (x >= 0) & (x < extent_x) & (y >= 0) & (y < extent_y)
     east_up, east_down = jnp.maximum(east, 0.0), jnp.minimum(east, 0.0)
     north_up, north_down = jnp.maximum(north, 0.0), jnp.minimum(north, 0.0)
+    snow = jnp.where(inside, snow, 0.0)
     for step in range(STEPS):
         before_x = pltpu.roll(snow, 1, 0)
         after_x = pltpu.roll(snow, shape[0] - 1, 0)
@@ -324,224 +326,306 @@
     lax.fori_loop(1, layers, body, first, unroll=7)
 
 
-def start_kernel(
-    devices, columns, temp_ref, rho_ref, pile_row_ref, pile_col_ref, own_ref, next_ref,
-    elink_ref, dprime_ref, rprime_ref, message_ref, own_rank_ref, next_rank_ref,
-    holder_ref, hit_ref, count_ref, a_ref, b_ref, p0_ref, p1_ref,
+def peer_id(peer, tiles_y):
+    return {"gx": lax.div(peer, tiles_y), "gy": lax.rem(peer, tiles_y)}
+
+
+def row_copy(send_ref, got_ref, sems, source, target, device, tiles_y):
+    return pltpu.make_async_remote_copy(
+        src_ref=send_ref.at[source],
+        dst_ref=got_ref.at[target],
+        send_sem=sems.at[0],
+        recv_sem=sems.at[1],
+        device_id=peer_id(device, tiles_y),
+        device_id_type=pl.DeviceIdType.MESH,
+    )
+
+
+def send_rows(send_ref, got_ref, sems, me, devices, tiles_y):
+    def body(step, carry):
+        peer = lax.rem(me + step, devices)
+        row_copy(send_ref, got_ref, sems, peer, me, peer, tiles_y).start()
+        return carry
+
+    lax.fori_loop(1, devices, body, 0)
+
+
+def rows_all(send_ref, got_ref, sems, me, devices, tiles_y):
+    every = pl.ds(0, devices - 1)
+    return row_copy(send_ref, got_ref, sems, every, every, lax.rem(me + 1, devices), tiles_y)
+
+
+def got_rows(send_ref, got_ref, sems, me, devices, tiles_y):
+    rows_all(send_ref, got_ref, sems, me, devices, tiles_y).wait_recv()
+    got_ref[pl.ds(me, 1)] = send_ref[pl.ds(me, 1)]
+
+
+def pack_sides(fields, strip_ref):
+    shape = fields[0].shape
+    lane = lanes_of(shape)
+    packed = jnp.zeros(shape, jnp.float32)
+    for f, field in enumerate(fields):
+        first = 4 * f
+        last = 16 + 4 * f
+        moved = pltpu.roll(field, first, 1) if first else field
+        packed = jnp.where((lane >= first) & (lane < first + STEPS), moved, packed)
+        moved = pltpu.roll(field, STEPS + last, 1)
+        packed = jnp.where((lane >= last) & (lane < last + STEPS), moved, packed)
+    strip_ref[...] = packed
+
+
+def joined_fields(fields, before_x, after_x, sides_after, sides_before):
+    lane = lanes_of(sides_after.shape)
+    out = []
+    for f, field in enumerate(fields):
+        ends = jnp.where(rows_of(after_x[f].shape) < STEPS, after_x[f], before_x[f])
+        core = jnp.concatenate([field, ends], axis=0)
+        first = 4 * f
+        last = 16 + 4 * f
+        after_y = pltpu.roll(sides_after, LANES - first, 1) if first else sides_after
+        before_y = pltpu.roll(sides_before, LANES - STEPS - last, 1)
+        side = jnp.where(lane < STEPS, after_y, jnp.where(lane >= LANES - STEPS, before_y, 0.0))
+        out.append(jnp.concatenate([core, side], axis=1))
+    return out
+
+
+def step_kernel(
+    tiles_x, tiles_y,
+    temp_hbm, rho_hbm, size_hbm, fluid_hbm, tally_ref, air_ref, factor_ref, snow_ref, east_ref,
+    north_ref, deep_temp_ref, deep_rho_ref, pile_ref, code_ref, index_hbm,
+    drift_ref, fresh_hbm, kept_hbm, deep_ref, arrival_ref,
+    temp_ref, rho_ref, size_ref, fluid_ref, own_ref, next_ref, ratio_ref, value_ref,
+    elink_ref, dprime_ref, rprime_ref, strip_x_ref, strip_y_ref, got_x_ref, got_y_ref, got_d_ref,
+    deep_send, deep_got, place_send, place_got, answer_send, answer_got, run_send, run_got,
+    hit_ref, count_ref, own_rank_ref, next_rank_ref, own_holder_ref, next_holder_ref,
+    own_b_ref, next_b_ref, code_b_ref, end_b_ref, a_ref, high_ref, low_ref, end_high_ref,
+    end_low_ref, p0_ref, p1_ref, p2_ref, in_sems, out_sems, halo_send, halo_got, deep_sems,
+    place_sems, answer_sems, run_sems,
 ):
-    diag, rhs = deep_eliminate(temp_ref, rho_ref, elink_ref, dprime_ref, rprime_ref)
-    message_ref[:, 0:LANES] = deep_message(
-        diag, rhs, pile_row_ref[...], pile_col_ref[...], columns, devices
-    )
+    devices = tiles_x * tiles_y
+    tile_x, tile_y = tally_ref.shape
+    columns = tile_x * tile_y
     rows = own_ref.shape[0]
     reaches = rows * LANES
-    peer = reaches // devices
-    holder_ref[...] = quotient(next_ref[...], reaches)
-    ranks(holder_ref, next_rank_ref, hit_ref, count_ref, devices, rows)
-    holder_ref[...] = quotient(own_ref[...], reaches)
-    ranks(holder_ref, own_rank_ref, hit_ref, count_ref, devices, rows)
-    position = remainder(own_ref[...], reaches)
-    p0_ref[...] = quotient(position, LANES).astype(jnp.float32)
-    p1_ref[...] = remainder(position, LANES).astype(jnp.float32)
-    fill_places(b_ref, own_rank_ref, peer, rows)
-    fill_values(a_ref, holder_ref, (p0_ref, p1_ref), devices, rows)
-    high, low = placed_sum(a_ref, b_ref, devices, peer, reaches, 2)
-    message_ref[:, LANES : LANES + peer] = high * LANES + low
-
-
-def middle_kernel(
-    devices, extents, origin_ref, snow_ref, east_ref, north_ref, temp_ref, rho_ref, size_ref,
-    fluid_ref, tally_ref, air_ref, factor_ref, code_ref, own_ref, next_ref, own_rank_ref,
-    next_rank_ref, got_ref, drift_ref, fresh_ref, kept_ref, answer_ref, ratio_ref, value_ref,
-    a_ref, b_ref, high_ref, low_ref, p0_ref, p1_ref, p2_ref,
-):
-    tile_x, tile_y = tally_ref.shape
+    gx, gy = lax.axis_index("gx"), lax.axis_index("gy")
+    me = gx * tiles_y + gy
+    follow = jnp.minimum(gx + 1, tiles_x - 1) * tiles_y + gy
+
+    barrier = pltpu.get_barrier_semaphore()
+
+    def greet(step, carry):
+        pl.semaphore_signal(
+            barrier, inc=1, device_id=peer_id(lax.rem(me + step, devices), tiles_y),
+            device_id_type=pl.DeviceIdType.MESH,
+        )
+        return carry
+
+    lax.fori_loop(1, devices, greet, 0)
+    loads = [
+        pltpu.make_async_copy(source, target, in_sems.at[k])
+        for k, (source, target) in enumerate(
+            (
+                (index_hbm.at[pl.ds(pl.multiple_of(me * rows, 8), rows)], own_ref),
+                (index_hbm.at[pl.ds(pl.multiple_of(follow * rows, 8), rows)], next_ref),
+                (temp_hbm, temp_ref),
+                (rho_hbm, rho_ref),
+                (size_hbm, size_ref),
+                (fluid_hbm, fluid_ref),
+            )
+        )
+    ]
+    for load in loads:
+        load.start()
+
+    edge = 2 * STEPS
+    fields = (snow_ref[...], east_ref[...], north_ref[...])
+    for f, field in enumerate(fields):
+        strip_x_ref[0, f] = field[0:edge]
+        strip_x_ref[1, f] = field[tile_x - edge : tile_x]
+    pack_sides(fields, strip_y_ref)
+    diag, rhs = deep_eliminate(deep_temp_ref, deep_rho_ref, elink_ref, dprime_ref, rprime_ref)
+    owner_row, owner_col, cell, position = deep_positions(pile_ref[...], columns)
+    deep_send[:, 0, :] = deep_message(diag, rhs, owner_row, cell, position, devices)
+
+    pl.semaphore_wait(barrier, devices - 1)
+    up_x, down_x = lax.rem(gx + 1, tiles_x), lax.rem(gx + tiles_x - 1, tiles_x)
+    up_y, down_y = lax.rem(gy + 1, tiles_y), lax.rem(gy + tiles_y - 1, tiles_y)
+    head = strip_y_ref.at[pl.ds(0, edge)]
+    tail = strip_y_ref.at[pl.ds(tile_x - edge, edge)]
+    halos = [
+        pltpu.make_async_remote_copy(
+            src_ref=source, dst_ref=target, send_sem=halo_send.at[k], recv_sem=halo_got.at[k],
+            device_id={"gx": x, "gy": y}, device_id_type=pl.DeviceIdType.MESH,
+        )
+        for k, (source, target, x, y) in enumerate(
+            (
+                (strip_x_ref.at[1], got_x_ref.at[0], up_x, gy),
+                (strip_x_ref.at[0], got_x_ref.at[1], down_x, gy),
+                (strip_y_ref, got_y_ref.at[0], gx, up_y),
+                (strip_y_ref, got_y_ref.at[1], gx, down_y),
+                (tail, got_d_ref.at[0], up_x, up_y),
+                (tail, got_d_ref.at[1], up_x, down_y),
+                (head, got_d_ref.at[2], down_x, up_y),
+                (head, got_d_ref.at[3], down_x, down_y),
+            )
+        )
+    ]
+    for halo in halos:
+        halo.start()
+    send_rows(deep_send, deep_got, deep_sems, me, devices, tiles_y)
+
+    loads[0].wait()
+    loads[1].wait()
+    own_holder_ref[...] = quotient(own_ref[...], reaches)
+    next_holder_ref[...] = quotient(next_ref[...], reaches)
+    ranks(own_holder_ref, own_rank_ref, hit_ref, count_ref, devices, rows)
+    fill_places(own_b_ref, own_rank_ref, LANES, rows)
+    spot = remainder(own_ref[...], reaches)
+    p0_ref[0:rows, :] = quotient(spot, LANES).astype(jnp.float32)
+    p1_ref[0:rows, :] = remainder(spot, LANES).astype(jnp.float32)
+    fill_values(a_ref, own_holder_ref, (p0_ref, p1_ref), devices, rows)
+    high, low = placed_sum(a_ref, own_b_ref, devices, LANES, reaches, 2)
+    place_send[:, 0, :] = high * LANES + low
+    send_rows(place_send, place_got, place_sems, me, devices, tiles_y)
+
+    for halo in halos:
+        halo.wait_recv()
+    near = rows_of((edge, LANES)) < STEPS
+    corner_after = jnp.where(near, got_d_ref[3], got_d_ref[1])
+    corner_before = jnp.where(near, got_d_ref[2], got_d_ref[0])
+    snow, east, north = joined_fields(
+        fields,
+        [got_x_ref[0, f] for f in range(3)],
+        [got_x_ref[1, f] for f in range(3)],
+        jnp.concatenate([got_y_ref[1], corner_after], axis=0),
+        jnp.concatenate([got_y_ref[0], corner_before], axis=0),
+    )
     snow = drift(
-        snow_ref[...], east_ref[...], north_ref[...], tile_x, tile_y,
-        origin_ref[0], origin_ref[1], extents[0], extents[1], STEPS,
+        snow, east, north, tile_x, tile_y, gx * tile_x, gy * tile_y,
+        tile_x * tiles_x, tile_y * tiles_y, STEPS,
     )
     drift_ref[...] = snow
     exchange = factor_ref[...] / (1.0 + snow)
     tally = tally_ref[...]
+    for load in loads[2:]:
+        load.wait()
     carry = eliminate(
         temp_ref, rho_ref, size_ref, tally, exchange, air_ref[...], ratio_ref, value_ref
     )
-    high, low, base_diag, base_rhs, flag = deep_places(got_ref[...], tile_x, tile_y)
+
+    got_rows(deep_send, deep_got, deep_sems, me, devices, tiles_y)
+    high, low, base_diag, base_rhs, flag = deep_places(deep_got[:, 0, :], tile_x, tile_y)
     bottom, surface_deep = bottom_row(temp_ref, tally, carry, base_diag, base_rhs, flag)
-    answer_ref[:, 0:LANES] = deep_answers(high, low, surface_deep, devices)
-    substitute(fresh_ref, ratio_ref, value_ref, bottom)
-    runoff = seep(fresh_ref, rho_ref, fluid_ref, tally, kept_ref)
-    rows = own_ref.shape[0]
-    reaches = rows * LANES
-    peer = reaches // devices
+    answer_send[:, 0, :] = deep_answers(high, low, surface_deep, devices)
+    send_rows(answer_send, answer_got, answer_sems, me, devices, tiles_y)
+
+    substitute(value_ref, ratio_ref, value_ref, bottom)
+    fresh_out = pltpu.make_async_copy(value_ref, fresh_hbm, out_sems.at[0])
+    fresh_out.start()
+    runoff = seep(value_ref, rho_ref, fluid_ref, tally, fluid_ref)
+    kept_out = pltpu.make_async_copy(fluid_ref, kept_hbm, out_sems.at[1])
+    kept_out.start()
+
     parts = (p0_ref, p1_ref, p2_ref)
-    split_three(runoff, parts)
+    ranks(next_holder_ref, next_rank_ref, hit_ref, count_ref, devices, rows)
+    fill_places(next_b_ref, next_rank_ref, LANES, rows)
     high_ref[...] = quotient(code_ref[...], LANES)
     low_ref[...] = remainder(code_ref[...], LANES)
-    fill_places(b_ref, low_ref, LANES, tile_x)
+    fill_places(code_b_ref, low_ref, LANES, tile_x)
+    split_three(runoff, parts)
     fill_values(a_ref, high_ref, parts, 2 * rows, tile_x)
-    binned = sum(placed_sum(a_ref, b_ref, 2 * rows, LANES, tile_x * LANES, 3))
+    binned = sum(placed_sum(a_ref, code_b_ref, 2 * rows, LANES, columns, 3))
     split_three(binned, parts)
-    for half, (slot_ref, rank_ref) in enumerate(((own_ref, own_rank_ref), (next_ref, next_rank_ref))):
-        high_ref[0:rows, :] = quotient(slot_ref[...], reaches)
-        fill_places(b_ref, rank_ref, peer, rows)
+    for half, (holder_ref, b_ref) in enumerate(
+        ((own_holder_ref, own_b_ref), (next_holder_ref, next_b_ref))
+    ):
         halves = [p.at[pl.ds(half * rows, rows)] for p in parts]
-        fill_values(a_ref, high_ref, halves, devices, rows)
-        lane = LANES + half * peer
-        answer_ref[:, lane : lane + peer] = sum(placed_sum(a_ref, b_ref, devices, peer, reaches, 3))
-
-
-def end_kernel(
-    devices, columns, returned_ref, pile_row_ref, pile_col_ref, elink_ref, dprime_in, rprime_in,
-    value_ref, place_ref, deep_ref, arrival_ref, dprime_ref, rprime_ref, a_ref, b_ref, high_ref,
-    low_ref, p0_ref, p1_ref, p2_ref,
-):
-    owner_row, owner_col, position = deep_positions(pile_row_ref[...], pile_col_ref[...], columns)
-    first = deep_return(returned_ref[...], owner_col, position, devices)
-    dprime_ref[...] = dprime_in[...]
-    rprime_ref[...] = rprime_in[...]
+        fill_values(a_ref, holder_ref, halves, devices, rows)
+        run_send[:, 0, half * LANES : (half + 1) * LANES] = sum(
+            placed_sum(a_ref, b_ref, devices, LANES, reaches, 3)
+        )
+    send_rows(run_send, run_got, run_sems, me, devices, tiles_y)
+
+    got_rows(answer_send, answer_got, answer_sems, me, devices, tiles_y)
+    first = deep_return(answer_got[:, 0, :], owner_col, position, devices)
     deep_substitute(first, elink_ref, dprime_ref, rprime_ref, deep_ref)
-    rows = value_ref.shape[0]
-    parts = (p0_ref, p1_ref, p2_ref)
-    split_three(value_ref[...], parts)
-    place = place_ref[...]
-    high_ref[...] = quotient(place, LANES)
-    low_ref[...] = remainder(place, LANES)
-    fill_places(b_ref, low_ref, LANES, rows)
-    fill_values(a_ref, high_ref, parts, rows, rows)
-    arrival_ref[...] = sum(placed_sum(a_ref, b_ref, rows, LANES, rows * LANES, 3))
-
-
-def call(kernel, outs, scratch, smem_first=False):
-    def run(*args):
-        specs = [pl.BlockSpec(memory_space=pltpu.VMEM)] * len(args)
-        if smem_first:
-            specs[0] = pl.BlockSpec(memory_space=pltpu.SMEM)
-        return pl.pallas_call(
-            kernel,
-            out_shape=[jax.ShapeDtypeStruct(s, d) for s, d in outs],
-            in_specs=specs,
-            out_specs=[pl.BlockSpec(memory_space=pltpu.VMEM)] * len(outs),
-            scratch_shapes=[pltpu.VMEM(s, d) for s, d in scratch],
-            compiler_params=pltpu.CompilerParams(vmem_limit_bytes=48 * 2**20),
-        )(*args)
-
-    return run
-
-
-def halo_of(cells, axis, dim, width):
-    count = lax.axis_size(axis)
-    head = lax.slice_in_dim(cells, 0, width, axis=dim)
-    tail = lax.slice_in_dim(cells, cells.shape[dim] - width, cells.shape[dim], axis=dim)
-    before = lax.ppermute(tail, axis, [(i, i + 1) for i in range(count - 1)])
-    after = lax.ppermute(head, axis, [(i + 1, i) for i in range(count - 1)])
-    gap = list(cells.shape)
-    gap[dim] = (-(cells.shape[dim] + 2 * width)) % (LANES if dim == 2 else 8)
-    return jnp.concatenate([cells, after, jnp.zeros(gap, cells.dtype), before], axis=dim)
-
-
-def local(
-    stratum_warmth_celsius,
-    stratum_mass_per_volume,
-    stratum_melt_fluid,
-    stratum_crystal_size,
-    pile_stratum_tally,
-    pile_atmospheric_warmth,
-    topmost_thermal_factor,
-    movable_topmost_powder,
-    first_axis_gust_fraction,
-    second_axis_gust_fraction,
-    extra_stratum_warmth,
-    extra_stratum_mass_per_volume,
-    parent_pile,
-    pile_stream_segment,
-    segment_result_index,
-):
+    got_rows(place_send, place_got, place_sems, me, devices, tiles_y)
+    place = place_got[:, 0, :].astype(jnp.int32)
+    end_high_ref[...] = quotient(place, LANES)
+    end_low_ref[...] = remainder(place, LANES)
+    fill_places(end_b_ref, end_low_ref, LANES, devices)
+    got_rows(run_send, run_got, run_sems, me, devices, tiles_y)
+    behind = pltpu.roll(run_got[:, 0, LANES:], tiles_y, 0)
+    behind = jnp.where(rows_of(behind.shape) >= tiles_y, behind, 0.0)
+    ends = [p.at[pl.ds(0, devices)] for p in parts]
+    split_three(run_got[:, 0, 0:LANES] + behind, ends)
+    fill_values(a_ref, end_high_ref, ends, rows, devices)
+    arrival_ref[...] = sum(placed_sum(a_ref, end_b_ref, rows, LANES, devices * LANES, 3))
+
+    for halo in halos:
+        halo.wait_send()
+    for send_ref, got_ref, sems in (
+        (deep_send, deep_got, deep_sems), (place_send, place_got, place_sems),
+        (answer_send, answer_got, answer_sems), (run_send, run_got, run_sems),
+    ):
+        rows_all(send_ref, got_ref, sems, me, devices, tiles_y).wait_send()
+    fresh_out.wait()
+    kept_out.wait()
+
+
+def local(*args):
     f32, i32, bf16 = jnp.float32, jnp.int32, jnp.bfloat16
-    layers, tile_x, tile_y = stratum_warmth_celsius.shape
-    deep_layers, slots = extra_stratum_warmth.shape
+    layers, tile_x, tile_y = args[0].shape
+    deep_layers, slots = args[10].shape
     tiles_x = lax.axis_size("gx")
     tiles_y = lax.axis_size("gy")
     devices = tiles_x * tiles_y
     columns = tile_x * tile_y
-    reaches = segment_result_index.shape[0] // devices
+    reaches = args[14].shape[0] // devices
     rows = reaches // LANES
-    peer = reaches // devices
-    extents = (tile_x * tiles_x, tile_y * tiles_y)
-    gx, gy = lax.axis_index("gx"), lax.axis_index("gy")
-    tile = gx * tiles_y + gy
-    after = jnp.minimum(gx + 1, tiles_x - 1) * tiles_y + gy
-    index = segment_result_index.reshape(devices * rows, LANES)
-    own = lax.dynamic_slice_in_dim(index, tile * rows, rows, axis=0)
-    following = lax.dynamic_slice_in_dim(index, after * rows, rows, axis=0)
-    pile_row = parent_pile.reshape(1, slots)
-    pile_col = parent_pile.reshape(slots, 1)
-
-    fields = jnp.stack([movable_topmost_powder, first_axis_gust_fraction, second_axis_gust_fraction])
-    fields = halo_of(fields, "gx", 1, STEPS)
-    fields = halo_of(fields, "gy", 2, STEPS)
-
+    strata = (layers, tile_x, tile_y)
+    deep = (deep_layers, slots)
+    edge = 2 * STEPS
     wide = max(3 * 2 * rows, 3 * devices)
-    elink, dprime, rprime, message, own_rank, next_rank = call(
-        functools.partial(start_kernel, devices, columns),
-        [((deep_layers, slots), f32)] * 3
-        + [((devices, LANES + peer), f32), ((rows, LANES), i32), ((rows, LANES), i32)],
-        [
-            ((rows, LANES), i32),
-            ((rows * devices, LANES), bf16),
-            ((rows * devices, 2 * LANES), f32),
-            ((2 * devices, reaches), bf16),
-            ((peer, reaches), bf16),
-            ((rows, LANES), f32),
-            ((rows, LANES), f32),
-        ],
-    )(extra_stratum_warmth, extra_stratum_mass_per_volume, pile_row, pile_col, own, following)
-    got = lax.all_to_all(message, ("gx", "gy"), split_axis=0, concat_axis=0, tiled=True)
-    origin = jnp.stack([gx * tile_x, gy * tile_y]).astype(i32)
-    drift_final, fresh, kept, answer = call(
-        functools.partial(middle_kernel, devices, extents),
-        [
-            ((tile_x, tile_y), f32),
-            ((layers, tile_x, tile_y), f32),
-            ((layers, tile_x, tile_y), f32),
-            ((devices, LANES + 2 * peer), f32),
-        ],
-        [
-            ((layers, tile_x, tile_y), f32),
-            ((layers, tile_x, tile_y), f32),
-            ((wide, columns), bf16),
-            ((LANES, columns), bf16),
-            ((tile_x, LANES), i32),
-            ((tile_x, LANES), i32),
-        ]
-        + [((tile_x, LANES), f32)] * 3,
-        smem_first=True,
+    width = max(columns, devices * LANES)
+    tall = max(tile_x, 2 * rows, devices)
+    grid = (rows, LANES)
+    message = (devices, 1, LANES)
+    scratch = (
+        [(strata, f32)] * 4
+        + [(grid, i32)] * 2
+        + [(strata, f32)] * 2
+        + [(deep, f32)] * 3
+        + [((2, 3, edge, tile_y), f32), ((tile_x, tile_y), f32), ((2, 3, edge, tile_y), f32)]
+        + [((2, tile_x, tile_y), f32), ((4, edge, tile_y), f32)]
+        + [(message, f32)] * 6
+        + [((devices, 1, 2 * LANES), f32)] * 2
+        + [((rows * devices, LANES), bf16), ((rows * devices, 2 * LANES), f32)]
+        + [(grid, i32)] * 4
+        + [((LANES, reaches), bf16)] * 2
+        + [((LANES, columns), bf16), ((LANES, devices * LANES), bf16), ((wide, width), bf16)]
+        + [((tile_x, tile_y), i32)] * 2
+        + [((devices, LANES), i32)] * 2
+        + [((tall, LANES), f32)] * 3
+    )
+    dma = pltpu.SemaphoreType.DMA
+    vmem = pl.BlockSpec(memory_space=pltpu.VMEM)
+    anywhere = pl.BlockSpec(memory_space=pl.ANY)
+    outs = ((tile_x, tile_y), strata, strata, deep, grid)
+    drift_final, fresh, kept, deep_fresh, arrival = pl.pallas_call(
+        functools.partial(step_kernel, tiles_x, tiles_y),
+        out_shape=[jax.ShapeDtypeStruct(s, f32) for s in outs],
+        in_specs=[anywhere] * 4 + [vmem] * 10 + [anywhere],
+        out_specs=[vmem, anywhere, anywhere, vmem, vmem],
+        scratch_shapes=[pltpu.VMEM(s, d) for s, d in scratch]
+        + [dma((6,)), dma((2,)), dma((8,)), dma((8,)), dma((2,)), dma((2,)), dma((2,)), dma((2,))],
+        compiler_params=pltpu.CompilerParams(
+            collective_id=0, has_side_effects=True, vmem_limit_bytes=56 * 2**20
+        ),
     )(
-        origin, fields[0], fields[1], fields[2], stratum_warmth_celsius, stratum_mass_per_volume,
-        stratum_crystal_size, stratum_melt_fluid, pile_stratum_tally, pile_atmospheric_warmth,
-        topmost_thermal_factor, pile_stream_segment, own, following, own_rank, next_rank,
-        got[:, 0:LANES],
-    )
-    back = lax.all_to_all(answer, ("gx", "gy"), split_axis=0, concat_axis=0, tiled=True)
-    straight = back[:, LANES : LANES + peer]
-    shifted = back[: devices - tiles_y, LANES + peer :]
-    total = straight + jnp.pad(shifted, ((tiles_y, 0), (0, 0)))
-    place = got[:, LANES:].astype(i32)
-    deep_fresh, arrival = call(
-        functools.partial(end_kernel, devices, columns),
-        [((deep_layers, slots), f32), ((rows, LANES), f32)],
-        [
-            ((deep_layers, slots), f32),
-            ((deep_layers, slots), f32),
-            ((3 * rows, reaches), bf16),
-            ((LANES, reaches), bf16),
-            ((rows, LANES), i32),
-            ((rows, LANES), i32),
-        ]
-        + [((rows, LANES), f32)] * 3,
-    )(
-        back[:, 0:LANES], pile_row, pile_col, elink, dprime, rprime,
-        total.reshape(rows, LANES), place.reshape(rows, LANES),
+        args[0], args[1], args[3], args[2], args[4], args[5], args[6], args[7], args[8], args[9],
+        args[10], args[11], args[12].reshape(1, slots), args[13],
+        args[14].reshape(devices * rows, LANES),
     )
     return drift_final, fresh, kept, deep_fresh, arrival.reshape(reaches)
 

time: 64 us -> 38.9 us (0.61)
  starting transfers between devices: 18.1 us -> 0 us
  blocking collectives: 13.9 us -> 0 us
  Pallas kernels: 18.1 us -> 31.3 us
  other arithmetic: 2.69 us -> 0 us
  waiting for transfers between devices: 2.28 us -> 0 us
  local copies, waits for them, and re-layouts: 7.42 us -> 6.67 us
    all_to_all x1 -> x0, blocking collectives: 13.9 us -> none  [local(): lax.all_to_all(answer, ('gx', 'gy'), split_axis=0, concat_axis=0, tiled=T...]
    pallas_call x3 -> x1, Pallas kernels: 18.1 us -> 31.3 us  [local(): pl.pallas_call(functools.partial(step_kernel, tiles_x, tiles_y), out_shap...]
    ppermute x4 -> x0, starting transfers between devices: 10.2 us -> none  [the longest x2 7.58 us: halo_of(): before = lax.ppermute(tail, axis, [(i, i + 1) for i in range(count - 1)])]
    all_to_all x1 -> x0, starting transfers between devices: 7.91 us -> none  [local(): lax.all_to_all(message, ('gx', 'gy'), split_axis=0, concat_axis=0, tiled=...]
    ppermute x4 -> x0, waiting for transfers between devices: 2.27 us -> none  [the longest x2 1.18 us: halo_of(): before = lax.ppermute(tail, axis, [(i, i + 1) for i in range(count - 1)])]
    concatenate x2 -> x0, other arithmetic: 1.69 us -> none  [halo_of(): jnp.concatenate([cells, after, jnp.zeros(gap, cells.dtype), before], axis...]
    unnamed x24 -> x11, local copies, waits for them, and re-layouts: 5.03 us -> 6.67 us
    slice x1 -> x0, other arithmetic: 0.9 us -> none  [halo_of(): head = lax.slice_in_dim(cells, 0, width, axis=dim)]
  transfers between devices with their start and end apart: 5 -> 0, of which waited for: 2 -> 0; matrix products, arithmetic and copies ran while one was open for 6% -> 0% of each run, Pallas kernels for 5% -> 0%
where the time goes in v1:
time: 38.9 us; the launch traced here: 38.6 us
  Pallas kernels  31.3 us (80%)
  local copies, waits for them, and re-layouts  6.67 us (17%)
  between operations  0.65 us (2%)
    pallas_call x1, Pallas kernels, local(): pl.pallas_call(functools.partial(step_kernel, tiles_x, tiles_y), out_shap...  31.3 us
    unnamed x11, local copies, waits for them, and re-layouts  6.67 us

profile of v1, /device:TPU:0, one launch (start us, length us, event | category | flops | bytes accessed | tf_op | source)
XLA Modules:
  0.0 38.6 jit_solution(301109314836038961)
XLA Ops:
  0.6 31.3 %shard_map.182 = (f32[64,128]{1,0:T(8,128)}, f32[50,64,128]{2,1,0:T(8,128)}, f32[50,64,128]{2,1,0:T(8,128)}, f32[50,96]{1,0:T(8,128)}, f32[32,128]{1,0:T(8,128)}) custom-call(f32[50,64,128]{2,1,0:T(8,128)} %temp_hbm.1, f32[50,64,128]{2,1,0:T(8,128)} %rho_hbm.1, f32[50,64,128]{2,1,0:T(8,128)} %size_hbm.1, f32[50,64,128]{2,1,0:T(8,128)} %fluid_hbm.1, ...), custom_call_target="tpu_custom_call" | custom-call | tf_op jit(solution)/shard_map/pallas_call | solution.py:615
  32.0 1.4 %copy.25 = f32[64,128]{1,0:T(8,128)} copy(f32[64,128]{1,0:T(8,128)} %get-tuple-element.20) | data formatting | bytes 65536
  33.3 0.0 copy-start
  33.3 2.9 %copy.26 = f32[50,64,128]{2,1,0:T(8,128)} copy(f32[50,64,128]{2,1,0:T(8,128)} %get-tuple-element.21) | data formatting | bytes 3276800
  36.2 0.0 copy-done
  36.2 0.0 copy-start.1
  36.2 0.0 copy-start.2
  36.2 1.2 %copy.27 = f32[50,64,128]{2,1,0:T(8,128)} copy(f32[50,64,128]{2,1,0:T(8,128)S(1)} %copy-done) | data formatting | bytes 3276800
  37.4 0.0 copy-done.1
  37.4 0.6 %copy.28 = f32[50,96]{1,0:T(8,128)} copy(f32[50,96]{1,0:T(8,128)S(1)} %copy-done.1) | data formatting | bytes 38400
  38.0 0.0 copy-done.2
  38.0 0.6 %copy.29 = f32[4096]{0:T(1024)} copy(f32[4096]{0:T(1024)S(1)} %bitcast.4) | data formatting | bytes 32768
Async XLA Ops:
  33.3 2.9 %copy-start = (f32[50,64,128]{2,1,0:T(8,128)S(1)}, f32[50,64,128]{2,1,0:T(8,128)}, u32[]{:S(2)}) copy-start(f32[50,64,128]{2,1,0:T(8,128)} %get-tuple-element.22) | copy-start | bytes 4915204
  36.2 1.2 %copy-start.1 = (f32[50,96]{1,0:T(8,128)S(1)}, f32[50,96]{1,0:T(8,128)}, u32[]{:S(2)}) copy-start(f32[50,96]{1,0:T(8,128)} %get-tuple-element.23) | copy-start | bytes 57604
  36.2 1.8 %copy-start.2 = (f32[32,128]{1,0:T(8,128)S(1)}, f32[32,128]{1,0:T(8,128)}, u32[]{:S(2)}) copy-start(f32[32,128]{1,0:T(8,128)} %get-tuple-element.14) | copy-start | bytes 49156

commit v2 on v1

--- a/solution.py
+++ b/solution.py
@@ -347,7 +347,7 @@
         row_copy(send_ref, got_ref, sems, peer, me, peer, tiles_y).start()
         return carry
 
-    lax.fori_loop(1, devices, body, 0)
+    lax.fori_loop(1, devices, body, 0, unroll=4)
 
 
 def rows_all(send_ref, got_ref, sems, me, devices, tiles_y):
@@ -393,14 +393,13 @@
     tiles_x, tiles_y,
     temp_hbm, rho_hbm, size_hbm, fluid_hbm, tally_ref, air_ref, factor_ref, snow_ref, east_ref,
     north_ref, deep_temp_ref, deep_rho_ref, pile_ref, code_ref, index_hbm,
-    drift_ref, fresh_hbm, kept_hbm, deep_ref, arrival_ref,
+    drift_ref, fresh_hbm, kept_hbm, deep_ref, total_ref, place_ref,
     temp_ref, rho_ref, size_ref, fluid_ref, own_ref, next_ref, ratio_ref, value_ref,
     elink_ref, dprime_ref, rprime_ref, strip_x_ref, strip_y_ref, got_x_ref, got_y_ref, got_d_ref,
-    deep_send, deep_got, place_send, place_got, answer_send, answer_got, run_send, run_got,
+    deep_send, deep_got, answer_send, answer_got, run_send, run_got,
     hit_ref, count_ref, own_rank_ref, next_rank_ref, own_holder_ref, next_holder_ref,
-    own_b_ref, next_b_ref, code_b_ref, end_b_ref, a_ref, high_ref, low_ref, end_high_ref,
-    end_low_ref, p0_ref, p1_ref, p2_ref, in_sems, out_sems, halo_send, halo_got, deep_sems,
-    place_sems, answer_sems, run_sems,
+    own_b_ref, next_b_ref, code_b_ref, a_ref, high_ref, low_ref, p0_ref, p1_ref, p2_ref, in_sems, out_sems, halo_send, halo_got, deep_sems,
+    answer_sems, run_sems,
 ):
     devices = tiles_x * tiles_y
     tile_x, tile_y = tally_ref.shape
@@ -445,7 +444,7 @@
     pack_sides(fields, strip_y_ref)
     diag, rhs = deep_eliminate(deep_temp_ref, deep_rho_ref, elink_ref, dprime_ref, rprime_ref)
     owner_row, owner_col, cell, position = deep_positions(pile_ref[...], columns)
-    deep_send[:, 0, :] = deep_message(diag, rhs, owner_row, cell, position, devices)
+    deep_send[:, 0, 0:LANES] = deep_message(diag, rhs, owner_row, cell, position, devices)
 
     pl.semaphore_wait(barrier, devices - 1)
     up_x, down_x = lax.rem(gx + 1, tiles_x), lax.rem(gx + tiles_x - 1, tiles_x)
@@ -472,7 +471,6 @@
     ]
     for halo in halos:
         halo.start()
-    send_rows(deep_send, deep_got, deep_sems, me, devices, tiles_y)
 
     loads[0].wait()
     loads[1].wait()
@@ -485,8 +483,13 @@
     p1_ref[0:rows, :] = remainder(spot, LANES).astype(jnp.float32)
     fill_values(a_ref, own_holder_ref, (p0_ref, p1_ref), devices, rows)
     high, low = placed_sum(a_ref, own_b_ref, devices, LANES, reaches, 2)
-    place_send[:, 0, :] = high * LANES + low
-    send_rows(place_send, place_got, place_sems, me, devices, tiles_y)
+    deep_send[:, 0, LANES:] = high * LANES + low
+    send_rows(deep_send, deep_got, deep_sems, me, devices, tiles_y)
+    ranks(next_holder_ref, next_rank_ref, hit_ref, count_ref, devices, rows)
+    fill_places(next_b_ref, next_rank_ref, LANES, rows)
+    high_ref[...] = quotient(code_ref[...], LANES)
+    low_ref[...] = remainder(code_ref[...], LANES)
+    fill_places(code_b_ref, low_ref, LANES, tile_x)
 
     for halo in halos:
         halo.wait_recv()
@@ -514,7 +517,7 @@
     )
 
     got_rows(deep_send, deep_got, deep_sems, me, devices, tiles_y)
-    high, low, base_diag, base_rhs, flag = deep_places(deep_got[:, 0, :], tile_x, tile_y)
+    high, low, base_diag, base_rhs, flag = deep_places(deep_got[:, 0, 0:LANES], tile_x, tile_y)
     bottom, surface_deep = bottom_row(temp_ref, tally, carry, base_diag, base_rhs, flag)
     answer_send[:, 0, :] = deep_answers(high, low, surface_deep, devices)
     send_rows(answer_send, answer_got, answer_sems, me, devices, tiles_y)
@@ -527,11 +530,6 @@
     kept_out.start()
 
     parts = (p0_ref, p1_ref, p2_ref)
-    ranks(next_holder_ref, next_rank_ref, hit_ref, count_ref, devices, rows)
-    fill_places(next_b_ref, next_rank_ref, LANES, rows)
-    high_ref[...] = quotient(code_ref[...], LANES)
-    low_ref[...] = remainder(code_ref[...], LANES)
-    fill_places(code_b_ref, low_ref, LANES, tile_x)
     split_three(runoff, parts)
     fill_values(a_ref, high_ref, parts, 2 * rows, tile_x)
     binned = sum(placed_sum(a_ref, code_b_ref, 2 * rows, LANES, columns, 3))
@@ -549,28 +547,52 @@
     got_rows(answer_send, answer_got, answer_sems, me, devices, tiles_y)
     first = deep_return(answer_got[:, 0, :], owner_col, position, devices)
     deep_substitute(first, elink_ref, dprime_ref, rprime_ref, deep_ref)
-    got_rows(place_send, place_got, place_sems, me, devices, tiles_y)
-    place = place_got[:, 0, :].astype(jnp.int32)
-    end_high_ref[...] = quotient(place, LANES)
-    end_low_ref[...] = remainder(place, LANES)
-    fill_places(end_b_ref, end_low_ref, LANES, devices)
+    place_ref[...] = deep_got[:, 0, LANES:].astype(jnp.int32)
     got_rows(run_send, run_got, run_sems, me, devices, tiles_y)
     behind = pltpu.roll(run_got[:, 0, LANES:], tiles_y, 0)
     behind = jnp.where(rows_of(behind.shape) >= tiles_y, behind, 0.0)
-    ends = [p.at[pl.ds(0, devices)] for p in parts]
-    split_three(run_got[:, 0, 0:LANES] + behind, ends)
-    fill_values(a_ref, end_high_ref, ends, rows, devices)
-    arrival_ref[...] = sum(placed_sum(a_ref, end_b_ref, rows, LANES, devices * LANES, 3))
+    total_ref[...] = run_got[:, 0, 0:LANES] + behind
 
     for halo in halos:
         halo.wait_send()
     for send_ref, got_ref, sems in (
-        (deep_send, deep_got, deep_sems), (place_send, place_got, place_sems),
+        (deep_send, deep_got, deep_sems),
         (answer_send, answer_got, answer_sems), (run_send, run_got, run_sems),
     ):
         rows_all(send_ref, got_ref, sems, me, devices, tiles_y).wait_send()
     fresh_out.wait()
     kept_out.wait()
+
+
+def end_kernel(
+    pieces, fresh_in, kept_in, drift_in, deep_in, total_ref, place_ref,
+    fresh_out, kept_out, drift_out, deep_out, arrival_ref,
+    a_ref, b_ref, high_ref, low_ref, p0_ref, p1_ref, p2_ref, sems,
+):
+    layers = fresh_in.shape[0]
+    depth = layers // pieces
+    spans = [pl.ds(k * depth, depth) for k in range(pieces)]
+    pairs = [(drift_in, drift_out), (deep_in, deep_out)]
+    pairs += [(fresh_in.at[span], fresh_out.at[span]) for span in spans]
+    pairs += [(kept_in.at[span], kept_out.at[span]) for span in spans]
+    copies = [
+        pltpu.make_async_copy(source, target, sems.at[k])
+        for k, (source, target) in enumerate(pairs)
+    ]
+    for copy in copies:
+        copy.start()
+    rows = arrival_ref.shape[0]
+    devices = total_ref.shape[0]
+    place = place_ref[...]
+    high_ref[...] = quotient(place, LANES)
+    low_ref[...] = remainder(place, LANES)
+    fill_places(b_ref, low_ref, LANES, devices)
+    parts = (p0_ref, p1_ref, p2_ref)
+    split_three(total_ref[...], parts)
+    fill_values(a_ref, high_ref, parts, rows, devices)
+    arrival_ref[...] = sum(placed_sum(a_ref, b_ref, rows, LANES, devices * LANES, 3))
+    for copy in copies:
+        copy.wait()
 
 
 def local(*args):
@@ -587,8 +609,9 @@
     deep = (deep_layers, slots)
     edge = 2 * STEPS
     wide = max(3 * 2 * rows, 3 * devices)
-    width = max(columns, devices * LANES)
-    tall = max(tile_x, 2 * rows, devices)
+    spread = (devices, LANES)
+    pieces = 5 if layers % 5 == 0 else 1
+    tall = max(tile_x, 2 * rows)
     grid = (rows, LANES)
     message = (devices, 1, LANES)
     scratch = (
@@ -598,27 +621,27 @@
         + [(deep, f32)] * 3
         + [((2, 3, edge, tile_y), f32), ((tile_x, tile_y), f32), ((2, 3, edge, tile_y), f32)]
         + [((2, tile_x, tile_y), f32), ((4, edge, tile_y), f32)]
-        + [(message, f32)] * 6
+        + [((devices, 1, 2 * LANES), f32)] * 2
+        + [(message, f32)] * 2
         + [((devices, 1, 2 * LANES), f32)] * 2
         + [((rows * devices, LANES), bf16), ((rows * devices, 2 * LANES), f32)]
         + [(grid, i32)] * 4
         + [((LANES, reaches), bf16)] * 2
-        + [((LANES, columns), bf16), ((LANES, devices * LANES), bf16), ((wide, width), bf16)]
+        + [((LANES, columns), bf16), ((wide, columns), bf16)]
         + [((tile_x, tile_y), i32)] * 2
-        + [((devices, LANES), i32)] * 2
         + [((tall, LANES), f32)] * 3
     )
     dma = pltpu.SemaphoreType.DMA
     vmem = pl.BlockSpec(memory_space=pltpu.VMEM)
     anywhere = pl.BlockSpec(memory_space=pl.ANY)
-    outs = ((tile_x, tile_y), strata, strata, deep, grid)
-    drift_final, fresh, kept, deep_fresh, arrival = pl.pallas_call(
+    outs = [((tile_x, tile_y), f32), (strata, f32), (strata, f32), (deep, f32), (spread, f32), (spread, i32)]
+    drift_final, fresh, kept, deep_fresh, total, place = pl.pallas_call(
         functools.partial(step_kernel, tiles_x, tiles_y),
-        out_shape=[jax.ShapeDtypeStruct(s, f32) for s in outs],
+        out_shape=[jax.ShapeDtypeStruct(s, d) for s, d in outs],
         in_specs=[anywhere] * 4 + [vmem] * 10 + [anywhere],
-        out_specs=[vmem, anywhere, anywhere, vmem, vmem],
+        out_specs=[vmem, anywhere, anywhere, vmem, vmem, vmem],
         scratch_shapes=[pltpu.VMEM(s, d) for s, d in scratch]
-        + [dma((6,)), dma((2,)), dma((8,)), dma((8,)), dma((2,)), dma((2,)), dma((2,)), dma((2,))],
+        + [dma((6,)), dma((2,)), dma((8,)), dma((8,)), dma((2,)), dma((2,)), dma((2,))],
         compiler_params=pltpu.CompilerParams(
             collective_id=0, has_side_effects=True, vmem_limit_bytes=56 * 2**20
         ),
@@ -627,6 +650,21 @@
         args[10], args[11], args[12].reshape(1, slots), args[13],
         args[14].reshape(devices * rows, LANES),
     )
+    ends = ((layers, tile_x, tile_y), strata, (tile_x, tile_y), deep, grid)
+    fresh, kept, drift_final, deep_fresh, arrival = pl.pallas_call(
+        functools.partial(end_kernel, pieces),
+        out_shape=[jax.ShapeDtypeStruct(s, f32) for s in ends],
+        in_specs=[anywhere] * 4 + [vmem] * 2,
+        out_specs=[anywhere] * 4 + [vmem],
+        scratch_shapes=[
+            pltpu.VMEM((3 * rows, devices * LANES), bf16),
+            pltpu.VMEM((LANES, devices * LANES), bf16),
+        ]
+        + [pltpu.VMEM(spread, i32)] * 2
+        + [pltpu.VMEM(spread, f32)] * 3
+        + [dma((2 + 2 * pieces,))],
+        compiler_params=pltpu.CompilerParams(vmem_limit_bytes=56 * 2**20),
+    )(fresh, kept, drift_final, deep_fresh, total, place)
     return drift_final, fresh, kept, deep_fresh, arrival.reshape(reaches)
 
 

time: 38.9 us -> 133 us (3.42)
  Pallas kernels: 31.3 us -> 132 us
  local copies, waits for them, and re-layouts: 6.67 us -> 0 us
    pallas_call x0 -> x1, Pallas kernels: none -> 104 us  [local(): pl.pallas_call(functools.partial(end_kernel, pieces), out_shape=[jax.Shap...]
    unnamed x11 -> x0, local copies, waits for them, and re-layouts: 6.67 us -> none
    pallas_call x1, Pallas kernels: 31.3 us -> 28.2 us  [local(): pl.pallas_call(functools.partial(step_kernel, tiles_x, tiles_y), out_shap...]
where the time goes in v2:
time: 133 us; the launch traced here: 132 us
  Pallas kernels  132 us (99%)
    pallas_call x1, Pallas kernels, local(): pl.pallas_call(functools.partial(end_kernel, pieces), out_shape=[jax.Shap...  104 us
    pallas_call x1, Pallas kernels, local(): pl.pallas_call(functools.partial(step_kernel, tiles_x, tiles_y), out_shap...  28.2 us

profile of v2, /device:TPU:0, one launch (start us, length us, event | category | flops | bytes accessed | tf_op | source)
XLA Modules:
  0.0 132.4 jit_solution(17463006567952375580)
XLA Ops:
  0.6 28.2 %shard_map.182 = (f32[64,128]{1,0:T(8,128)}, f32[50,64,128]{2,1,0:T(8,128)}, f32[50,64,128]{2,1,0:T(8,128)}, f32[50,96]{1,0:T(8,128)}, f32[32,128]{1,0:T(8,128)}, /*index=5*/s32[32,128]{1,0:T(8,128)}) custom-call(f32[50,64,128]{2,1,0:T(8,128)} %temp_hbm.1, f32[50,64,128]{2,1,0:T(8,128)} %rho_hbm.1, f32[50,64,128]{2,1,0:T(8,128)} %size_hbm.1, ...), custom_call_target="tpu_custom_call" | custom-call | tf_op jit(solution)/shard_map/pallas_call | solution.py:638
  28.8 103.6 %shard_map.183 = (f32[50,64,128]{2,1,0:T(8,128)}, f32[50,64,128]{2,1,0:T(8,128)}, f32[64,128]{1,0:T(8,128)}, f32[50,96]{1,0:T(8,128)}, f32[32,128]{1,0:T(8,128)}) custom-call(f32[50,64,128]{2,1,0:T(8,128)} %get-tuple-element.16.fresh_in, f32[50,64,128]{2,1,0:T(8,128)} %get-tuple-element.17.kept_in, f32[64,128]{1,0:T(8,128)} %get-tuple-element.18.drift_in, ...), custom_call_target="tpu_custom_call" | custom-call | tf_op jit(solution)/shard_map/pallas_call | solution.py:654

commit v3 on v2

--- a/solution.py
+++ b/solution.py
@@ -567,19 +567,25 @@
 def end_kernel(
     pieces, fresh_in, kept_in, drift_in, deep_in, total_ref, place_ref,
     fresh_out, kept_out, drift_out, deep_out, arrival_ref,
-    a_ref, b_ref, high_ref, low_ref, p0_ref, p1_ref, p2_ref, sems,
+    a_ref, b_ref, high_ref, low_ref, p0_ref, p1_ref, p2_ref,
+    fresh_ref, kept_ref, drift_ref, deep_ref, in_sems, out_sems,
 ):
     layers = fresh_in.shape[0]
     depth = layers // pieces
     spans = [pl.ds(k * depth, depth) for k in range(pieces)]
-    pairs = [(drift_in, drift_out), (deep_in, deep_out)]
-    pairs += [(fresh_in.at[span], fresh_out.at[span]) for span in spans]
-    pairs += [(kept_in.at[span], kept_out.at[span]) for span in spans]
-    copies = [
-        pltpu.make_async_copy(source, target, sems.at[k])
-        for k, (source, target) in enumerate(pairs)
+    trips = [(drift_in, drift_ref, drift_out), (deep_in, deep_ref, deep_out)]
+    for span in spans:
+        trips.append((fresh_in.at[span], fresh_ref.at[span], fresh_out.at[span]))
+        trips.append((kept_in.at[span], kept_ref.at[span], kept_out.at[span]))
+    inward = [
+        pltpu.make_async_copy(source, stop, in_sems.at[k])
+        for k, (source, stop, target) in enumerate(trips)
     ]
-    for copy in copies:
+    outward = [
+        pltpu.make_async_copy(stop, target, out_sems.at[k])
+        for k, (source, stop, target) in enumerate(trips)
+    ]
+    for copy in inward:
         copy.start()
     rows = arrival_ref.shape[0]
     devices = total_ref.shape[0]
@@ -587,11 +593,14 @@
     high_ref[...] = quotient(place, LANES)
     low_ref[...] = remainder(place, LANES)
     fill_places(b_ref, low_ref, LANES, devices)
+    for arrived, copy in zip(inward, outward):
+        arrived.wait()
+        copy.start()
     parts = (p0_ref, p1_ref, p2_ref)
     split_three(total_ref[...], parts)
     fill_values(a_ref, high_ref, parts, rows, devices)
     arrival_ref[...] = sum(placed_sum(a_ref, b_ref, rows, LANES, devices * LANES, 3))
-    for copy in copies:
+    for copy in outward:
         copy.wait()
 
 
@@ -662,7 +671,8 @@
         ]
         + [pltpu.VMEM(spread, i32)] * 2
         + [pltpu.VMEM(spread, f32)] * 3
-        + [dma((2 + 2 * pieces,))],
+        + [pltpu.VMEM(s, f32) for s in (strata, strata, (tile_x, tile_y), deep)]
+        + [dma((2 + 2 * pieces,))] * 2,
         compiler_params=pltpu.CompilerParams(vmem_limit_bytes=56 * 2**20),
     )(fresh, kept, drift_final, deep_fresh, total, place)
     return drift_final, fresh, kept, deep_fresh, arrival.reshape(reaches)

time: 133 us -> 33.4 us (0.25)
  Pallas kernels: 132 us -> 32.4 us
    pallas_call x1, Pallas kernels: 104 us -> 4.26 us  [local(): pl.pallas_call(functools.partial(end_kernel, pieces), out_shape=[jax.Shap...]
where the time goes in v3:
time: 33.4 us; the launch traced here: 33.1 us
  Pallas kernels  32.4 us (97%)
  between operations  0.65 us (2%)
    pallas_call x1, Pallas kernels, local(): pl.pallas_call(functools.partial(step_kernel, tiles_x, tiles_y), out_shap...  28.2 us
    pallas_call x1, Pallas kernels, local(): pl.pallas_call(functools.partial(end_kernel, pieces), out_shape=[jax.Shap...  4.26 us

profile of v3, /device:TPU:0, one launch (start us, length us, event | category | flops | bytes accessed | tf_op | source)
XLA Modules:
  0.0 33.1 jit_solution(8395102057038993008)
XLA Ops:
  0.6 28.2 %shard_map.182 = (f32[64,128]{1,0:T(8,128)}, f32[50,64,128]{2,1,0:T(8,128)}, f32[50,64,128]{2,1,0:T(8,128)}, f32[50,96]{1,0:T(8,128)}, f32[32,128]{1,0:T(8,128)}, /*index=5*/s32[32,128]{1,0:T(8,128)}) custom-call(f32[50,64,128]{2,1,0:T(8,128)} %temp_hbm.1, f32[50,64,128]{2,1,0:T(8,128)} %rho_hbm.1, f32[50,64,128]{2,1,0:T(8,128)} %size_hbm.1, ...), custom_call_target="tpu_custom_call" | custom-call | tf_op jit(solution)/shard_map/pallas_call | solution.py:647
  28.8 4.3 %shard_map.183 = (f32[50,64,128]{2,1,0:T(8,128)}, f32[50,64,128]{2,1,0:T(8,128)}, f32[64,128]{1,0:T(8,128)}, f32[50,96]{1,0:T(8,128)}, f32[32,128]{1,0:T(8,128)}) custom-call(f32[50,64,128]{2,1,0:T(8,128)} %get-tuple-element.16.fresh_in, f32[50,64,128]{2,1,0:T(8,128)} %get-tuple-element.17.kept_in, f32[64,128]{1,0:T(8,128)} %get-tuple-element.18.drift_in, ...), custom_call_target="tpu_custom_call" | custom-call | tf_op jit(solution)/shard_map/pallas_call | solution.py:663
